TPU v7x, 512 devices: a whole 4x8x8 slice. The times are simulated.
512 devices in a mesh: grid: 64 (over y, z_hi, core), hel: 8 (over z_lo, x).
Axes of the slice: x: 4, y: 8, z: 8 (z_hi: 4, z_lo: 2; z = z_hi * 2 + z_lo), core: 2. Of those that a mesh axis runs over, the one named last changes fastest.
Arguments:
- packet_prev: float32 [8, 1024, 5120], P('hel', 'grid'), may hold values from -6 to 6
- packet_now: float32 [8, 1024, 5120], P('hel', 'grid'), may hold values from -6 to 6
- angular_table: float32 [8, 1024, 1536], P('hel', None, 'grid'), may hold values from -0.15625 to 0.15625
- potential: float32 [1536, 5120], P(None, 'grid'), may hold values from 0 to 2
- rotation: float32 [8, 1024], P('hel', 'grid'), may hold values from 0.05 to 1
- radial_weight: float32 [64], replicated, may hold values from 0.5 to 2
- coupling: float32 [8, 1024], P('hel', 'grid'), may hold values from -0.6 to 0.6
- centrifugal: float32 [80], replicated, may hold values from 0.5 to 1.5
Outputs:
- packet_mid: float32 [8, 1024, 5120], P('hel', 'grid')
- packet_last: float32 [8, 1024, 5120], P('hel', 'grid')
All inputs are finite; a program needn't handle non-finite values.
Results may differ from a plain program's by a relative error of at most 0.0001.
Values sent between devices are 32-bit elements; how exact they have to be, the bound alone decides.
A program may use at most 128 MiB of HBM per device.

v0:
```python
import jax
import jax.numpy as jnp
from jax import lax
from jax.sharding import Mesh
from jax.sharding import PartitionSpec as P

RB = 80
RS = 64
STEPS = 2
GRID = ("grid_0", "grid_1", "grid_2")


big_scale = 0.05
small_scale = 0.08
centre = 1.0
half_width = 1.5


def in_order(parts, dim):
    parts = jnp.moveaxis(parts, 0, dim)
    lengths = parts.shape
    return parts.reshape(*lengths[:dim], lengths[dim] * lengths[dim + 1], *lengths[dim + 2 :])


def stacked_from(shard, axes, sequence):
    parts = shard[None]
    for k in sequence:
        parts = lax.all_gather(parts, axes[k], axis=0, tiled=True)
    carried = [lax.axis_size(axes[k]) for k in reversed(sequence)]
    parts = parts.reshape(*carried, *shard.shape)
    turned = sorted(range(len(sequence)), key=lambda place: sequence[len(sequence) - 1 - place])
    return parts.transpose(*turned, *range(len(sequence), parts.ndim)).reshape(-1, *shard.shape)


def whole_of(shard, axes, sequence, dim):
    return in_order(stacked_from(shard, axes, sequence), dim)


def from_behind(shard, axis, by):
    size = lax.axis_size(axis)
    pairs = [(i, i + by) for i in range(size) if 0 <= i + by < size]
    return lax.ppermute(shard, axis, pairs)


def kinetic(count, coef):
    index = jnp.arange(count)
    offset = index[:, None] - index[None, :]
    parity = (1 - 2 * (jnp.abs(offset) % 2)).astype(jnp.float32)
    square = jnp.maximum(offset * offset, 1).astype(jnp.float32)
    return coef * jnp.where(offset == 0, jnp.float32(jnp.pi**2 / 3.0), 2.0 * parity / square)


def shards(
    packet_prev,
    packet_now,
    angular_table,
    potential,
    rotation,
    radial_weight,
    coupling,
    centrifugal,
):
    high = lax.Precision.HIGHEST
    kin_big = kinetic(RB, big_scale)
    kin_small = kinetic(RS, small_scale)
    whole_table = whole_of(angular_table, GRID, (1, 0, 2), 2)[0]
    link = coupling[:, :, None] * jnp.repeat(centrifugal, RS)[None, None, :]
    rot_factor = rotation[:, :, None] * jnp.tile(radial_weight, RB)[None, None, :]
    older, newer = (packet_prev, packet_now)
    for step in range(STEPS):
        local_funcs = newer.shape[1]
        grid4 = newer.reshape(1, local_funcs, RB, RS)
        radial = jnp.einsum("ab,kjbs->kjas", kin_big, grid4, precision=high)
        radial = radial + jnp.einsum("st,kjat->kjas", kin_small, grid4, precision=high)
        radial = radial.reshape(newer.shape)
        below = from_behind(newer, "hel", 1)
        above = from_behind(link * newer, "hel", -1)
        spread = lax.all_to_all(newer[0], GRID, split_axis=1, concat_axis=0, tiled=True)
        points = lax.dot_general(whole_table, spread, (((0,), (0,)), ((), ())), precision=high)
        back = jnp.dot(whole_table, points * potential, precision=high)
        returned = lax.all_to_all(back, GRID, split_axis=0, concat_axis=1, tiled=True)[None]
        total = radial + rot_factor * newer + returned + link * below + above
        older, newer = (newer, 2.0 * ((total - centre * newer) / half_width) - older)
    return (older, newer)


def solution(mesh):
    finer = Mesh(
        mesh.devices.reshape(8, 4, 2, mesh.shape["hel"]), ("grid_0", "grid_1", "grid_2", "hel")
    )
    placed = (
        P("hel", GRID, None),
        P("hel", GRID, None),
        P("hel", None, GRID),
        P(None, GRID),
        P("hel", GRID),
        P(),
        P("hel", GRID),
        P(),
    )
    return jax.shard_map(
        shards,
        mesh=finer,
        in_specs=placed,
        out_specs=(P("hel", GRID, None), P("hel", GRID, None)),
        check_vma=False,
    )
```

profile of v0, /device:TPU:64, one launch (start us, length us, event | category | flops | bytes accessed | tf_op | source)
XLA Modules:
  0.0 240.3 jit_solution(2455111808099106749)
XLA Ops:
  7.2 22.3 %all-gather = f32[4,1024,24]{1,2,0:T(8,128)} all-gather(f32[1,1024,24]{1,2,0:T(8,128)} %param.10), channel_id=2, replica_groups=mesh['grid_0'=8,'grid_1'=4,'grid_2'=2,'hel'=8] {'grid_1'}, dimensions={0}, use_global_device_ids=true | all-gather | bytes 491520 | tf_op jit(solution)/shard_map/all_gather | solution.py:28
  29.6 46.1 %all-gather.6.cloned.1.call-done = f32[32,1024,24]{1,2,0:T(8,128)} async-done(((f32[4,1024,24]{1,2,0:T(8,128)}), f32[32,1024,24]{1,2,0:T(8,128)}) %all-gather.6.cloned.1.call-update) | async-done | bytes 3145744 | tf_op jit(solution)/shard_map/all_gather | solution.py:28
  75.7 1.2 all_to_all.52
  78.2 10.0 %all-to-all-start = ((f32[16,64,80]{2,0,1:T(8,128)}), f32[16,64,80]{2,0,1:T(8,128)S(1)}, u32[]{:S(2)}, u32[]{:S(2)}) async-start(f32[16,64,80]{2,0,1:T(8,128)} %copy.45), calls=%async_computation | async-start | bytes 1048576 | tf_op jit(solution)/shard_map/all_to_all | solution.py:78
  88.2 3.4 %collective-permute-start = (f32[1,16,5120]{2,1,0:T(8,128)S(1)}, f32[1,16,5120]{2,1,0:T(8,128)S(1)}, u32[]{:S(2)}, u32[]{:S(2)}) collective-permute-start(f32[1,16,5120]{2,1,0:T(8,128)S(1)} %copy-done.1), channel_id=1, source_target_pairs={{0,1},{1,2},{2,3},{3,4},{4,5},{5,6},{6,7},{8,9},{9,10},{10,11},{11... | collective-permute-start | bytes 983048 | tf_op jit(solution)/shard_map/ppermute | solution.py:42
  91.8 9.9 %all-gather.8.cloned.1.call-done = f32[64,1024,24]{1,2,0:T(8,128)} async-done(((f32[32,1024,24]{1,2,0:T(8,128)}), f32[64,1024,24]{1,2,0:T(8,128)}) %all-gather.8.cloned.1.call-update) | async-done | bytes 6291472 | tf_op jit(solution)/shard_map/all_gather | solution.py:28
  101.7 6.6 %copy.44 = f32[8,4,2,1,1024,24]{4,5,3,2,1,0:T(8,128)} copy(f32[8,4,2,1,1024,24]{4,5,3,1,0,2:T(8,128)} %bitcast.82) | data formatting | bytes 12582912 | tf_op jit(solution)/shard_map/transpose | solution.py:32
  108.3 8.0 %convolution_multiply_fusion = f32[1536,80]{0,1:T(8,128)S(1)} fusion(f32[1536,80]{0,1:T(8,128)S(1)} %copy-done.3, f32[1024,1536]{0,1:T(8,128)} %bitcast.76, f32[1024,80]{1,0:T(8,128)S(1)} %bitcast.87), kind=kOutput, calls=%fused_computation | convolution fusion | flops 1510072320 | bytes 7602176 | tf_op jit(solution)/shard_map/dot_general | solution.py:79
  116.4 3.9 %convolution_bitcast_fusion.5 = f32[1024,80]{0,1:T(8,128)S(1)} fusion(f32[1536,80]{0,1:T(8,128)S(1)} %convolution_multiply_fusion, f32[1024,1536]{0,1:T(8,128)S(1)} %bitcast.78), kind=kOutput, calls=%fused_computation.9 | convolution fusion | flops 1509949440 | bytes 7110656 | tf_op jit(solution)/shard_map/dot_general | solution.py:80
  121.3 12.4 %all-to-all-start.1 = ((f32[64,16,80]{2,1,0:T(8,128)}), f32[64,16,80]{2,1,0:T(8,128)S(1)}, u32[]{:S(2)}, u32[]{:S(2)}) async-start(f32[64,16,80]{2,1,0:T(8,128)} %bitcast.18), calls=%async_computation.1 | async-start | bytes 1048576 | tf_op jit(solution)/shard_map/all_to_all | solution.py:81
  134.6 5.5 %collective-permute-start.1 = (f32[1,16,5120]{2,1,0:T(8,128)}, f32[1,16,5120]{2,1,0:T(8,128)S(1)}, u32[]{:S(2)}, u32[]{:S(2)}) collective-permute-start(f32[1,16,5120]{2,1,0:T(8,128)} %multiply_multiply_fusion.2), channel_id=1, source_target_pairs={{1,0},{2,1},{3,2},{4,3},{5,4},{6,5},{7,6},{9,8},{10,9},{11,10},{12... | collective-permute-start | bytes 983048 | tf_op jit(solution)/shard_map/ppermute | solution.py:42
  141.1 1.7 fusion.1
  143.3 9.5 %all-to-all-done.1 = f32[64,16,80]{2,1,0:T(8,128)S(1)} async-done(((f32[64,16,80]{2,1,0:T(8,128)}), f32[64,16,80]{2,1,0:T(8,128)S(1)}, u32[]{:S(2)}, u32[]{:S(2)}) %all-to-all-start.1) | async-done | bytes 327712 | tf_op jit(solution)/shard_map/all_to_all | solution.py:81
  155.7 2.3 multiply_multiply_fusion
  158.5 29.8 %all_to_all.70 = f32[16,64,80]{2,0,1:T(8,128)S(1)} all-to-all(f32[16,64,80]{2,0,1:T(8,128)S(1)} %copy.51), channel_id=1, replica_groups=mesh['grid_0'=8,'grid_1'=4,'grid_2'=2,'hel'=8] {'grid_0','grid_1','grid_2'}, dimensions={1} | all-to-all | bytes 655360 | tf_op jit(solution)/shard_map/all_to_all | solution.py:78
  188.3 9.5 %fusion = f32[1536,80]{0,1:T(8,128)S(1)} fusion(f32[1536,80]{0,1:T(8,128)} %param.11, f32[1024,80]{1,0:T(8,128)S(1)} %bitcast.88, f32[1024,1536]{0,1:T(8,128)} %bitcast.77), kind=kOutput, calls=%fused_computation.2 | convolution fusion | flops 1510072320 | bytes 7602176 | tf_op jit(solution)/shard_map/dot_general | solution.py:79
  197.8 3.9 %convolution_bitcast_fusion.4 = f32[1024,80]{0,1:T(8,128)S(1)} fusion(f32[1536,80]{0,1:T(8,128)S(1)} %fusion, f32[1024,1536]{0,1:T(8,128)S(1)} %bitcast.81), kind=kOutput, calls=%fused_computation.8 | convolution fusion | flops 1509949440 | bytes 7110656 | tf_op jit(solution)/shard_map/dot_general | solution.py:80
  202.8 6.2 %all-to-all-start.3 = ((f32[64,16,80]{2,1,0:T(8,128)}), f32[64,16,80]{2,1,0:T(8,128)S(1)}, u32[]{:S(2)}, u32[]{:S(2)}) async-start(f32[64,16,80]{2,1,0:T(8,128)} %bitcast.31), calls=%async_computation.3 | async-start | bytes 1048576 | tf_op jit(solution)/shard_map/all_to_all | solution.py:81
  209.2 1.9 collective-permute-start.2
  211.1 6.6 %collective-permute-start.3 = (f32[1,16,5120]{2,1,0:T(8,128)S(1)}, f32[1,16,5120]{2,1,0:T(8,128)S(1)}, u32[]{:S(2)}, u32[]{:S(2)}) collective-permute-start(f32[1,16,5120]{2,1,0:T(8,128)S(1)} %copy-done.5), channel_id=1, source_target_pairs={{1,0},{2,1},{3,2},{4,3},{5,4},{6,5},{7,6},{9,8},{10,9},{11,10},{12... | collective-permute-start | bytes 983048 | tf_op jit(solution)/shard_map/ppermute | solution.py:42
  217.8 1.7 convolution_bitcast_fusion.1
  219.5 1.2 fusion.2
  221.1 7.0 %all-to-all-done.3 = f32[64,16,80]{2,1,0:T(8,128)S(1)} async-done(((f32[64,16,80]{2,1,0:T(8,128)}), f32[64,16,80]{2,1,0:T(8,128)S(1)}, u32[]{:S(2)}, u32[]{:S(2)}) %all-to-all-start.3) | async-done | bytes 327712 | tf_op jit(solution)/shard_map/all_to_all | solution.py:81
  228.6 3.9 %collective-permute-done.2 = f32[1,16,5120]{2,1,0:T(8,128)S(1)} collective-permute-done((f32[1,16,5120]{2,1,0:T(8,128)S(1)}, f32[1,16,5120]{2,1,0:T(8,128)S(1)}, u32[]{:S(2)}, u32[]{:S(2)}) %collective-permute-start.2) | collective-permute-done | bytes 327712 | tf_op jit(solution)/shard_map/ppermute | solution.py:42
  (58 shorter events, 11.2 us)
Async XLA Ops:
  7.2 81.0 %copy-start.1 = (f32[1,16,5120]{2,1,0:T(8,128)S(1)}, f32[1,16,5120]{2,1,0:T(8,128)}, u32[]{:S(2)}) copy-start(f32[1,16,5120]{2,1,0:T(8,128)} %param.9) | copy-start | bytes 983044
  7.2 84.4 %copy-start.9 = (f32[80]{0:T(128)S(1)}, f32[80]{0:T(128)}, u32[]{:S(2)}) copy-start(f32[80]{0:T(128)} %param.15) | copy-start | bytes 964
  7.2 68.5 %all-gather.6.cloned.1.call-start = ((), (), s32[]{:S(2)}) async-start(), calls=%async_computation.4 | async-start | bytes 3538944 | tf_op jit(solution)/shard_map/all_gather | solution.py:28
  29.5 72.2 %all-gather.8.cloned.1.call-start = ((), (), s32[]{:S(2)}) async-start(), calls=%async_computation.5 | async-start | bytes 9437184 | tf_op jit(solution)/shard_map/all_gather | solution.py:28
  78.2 30.1 %all-to-all-start = ((f32[16,64,80]{2,0,1:T(8,128)}), f32[16,64,80]{2,0,1:T(8,128)S(1)}, u32[]{:S(2)}, u32[]{:S(2)}) async-start(f32[16,64,80]{2,0,1:T(8,128)} %copy.45), calls=%async_computation | async-start | bytes 1048576 | tf_op jit(solution)/shard_map/all_to_all | solution.py:78
  88.2 66.0 %collective-permute-start = (f32[1,16,5120]{2,1,0:T(8,128)S(1)}, f32[1,16,5120]{2,1,0:T(8,128)S(1)}, u32[]{:S(2)}, u32[]{:S(2)}) collective-permute-start(f32[1,16,5120]{2,1,0:T(8,128)S(1)} %copy-done.1), channel_id=1, source_target_pairs={{0,1},{1,2},{2,3},{3,4},{4,5},{5,6},{6,7},{8,9},{9,10},{10,11},{11... | collective-permute-start | bytes 983048 | tf_op jit(solution)/shard_map/ppermute | solution.py:42
  101.7 6.6 %copy-start.3 = (f32[1536,80]{0,1:T(8,128)S(1)}, f32[1536,80]{0,1:T(8,128)}, u32[]{:S(2)}) copy-start(f32[1536,80]{0,1:T(8,128)} %param.11) | copy-start | bytes 1474564
  108.3 8.1 %copy-start = (f32[8,4,2,1,1024,24]{4,5,3,2,1,0:T(8,128)S(1)}, f32[8,4,2,1,1024,24]{4,5,3,2,1,0:T(8,128)}, u32[]{:S(2)}) copy-start(f32[8,4,2,1,1024,24]{4,5,3,2,1,0:T(8,128)} %copy.44) | copy-start | bytes 18874372
  116.4 17.4 %copy-start.7 = (f32[1,16]{1,0:T(1,128)S(1)}, f32[1,16]{1,0:T(1,128)}, u32[]{:S(2)}) copy-start(f32[1,16]{1,0:T(1,128)} %param.14) | copy-start | bytes 196
  120.3 23.0 %copy-start.10 = (f32[64]{0:T(128)S(1)}, f32[64]{0:T(128)}, u32[]{:S(2)}) copy-start(f32[64]{0:T(128)} %param.13) | copy-start | bytes 772
  120.3 35.4 %copy-start.8 = (f32[1,16]{1,0:T(1,128)S(1)}, f32[1,16]{1,0:T(1,128)}, u32[]{:S(2)}) copy-start(f32[1,16]{1,0:T(1,128)} %param.12) | copy-start | bytes 196
  121.3 31.5 %all-to-all-start.1 = ((f32[64,16,80]{2,1,0:T(8,128)}), f32[64,16,80]{2,1,0:T(8,128)S(1)}, u32[]{:S(2)}, u32[]{:S(2)}) async-start(f32[64,16,80]{2,1,0:T(8,128)} %bitcast.18), calls=%async_computation.1 | async-start | bytes 1048576 | tf_op jit(solution)/shard_map/all_to_all | solution.py:81
  134.6 19.6 %collective-permute-start.1 = (f32[1,16,5120]{2,1,0:T(8,128)}, f32[1,16,5120]{2,1,0:T(8,128)S(1)}, u32[]{:S(2)}, u32[]{:S(2)}) collective-permute-start(f32[1,16,5120]{2,1,0:T(8,128)} %multiply_multiply_fusion.2), channel_id=1, source_target_pairs={{1,0},{2,1},{3,2},{4,3},{5,4},{6,5},{7,6},{9,8},{10,9},{11,10},{12... | collective-permute-start | bytes 983048 | tf_op jit(solution)/shard_map/ppermute | solution.py:42
  154.2 0.7 copy-start.6
  154.9 0.7 copy-start.4
  155.7 42.2 %slice-start = ((s8[6291456]{0:T(1024)(128)(4,1)}), s8[2097152]{0:T(1024)(128)(4,1)S(1)}, s32[]{:S(2)}) async-start(s8[6291456]{0:T(1024)(128)(4,1)} %bitcast.79), calls=%async_computation.6 | async-start | bytes 4194304
  157.9 74.7 %copy-start.2 = (f32[1,16,5120]{2,1,0:T(8,128)}, f32[1,16,5120]{2,1,0:T(8,128)S(1)}, u32[]{:S(2)}) copy-start(f32[1,16,5120]{2,1,0:T(8,128)S(1)} %get-tuple-element.3) | copy-start | bytes 983044
  188.3 9.5 %slice-start.1 = ((s8[6291456]{0:T(1024)(128)(4,1)}), s8[4194304]{0:T(1024)(128)(4,1)S(1)}, s32[]{:S(2)}) async-start(s8[6291456]{0:T(1024)(128)(4,1)} %bitcast.79), calls=%async_computation.7 | async-start | bytes 8388608
  197.8 13.3 %copy-start.5 = (f32[1,16,5120]{2,1,0:T(8,128)S(1)}, f32[1,16,5120]{2,1,0:T(8,128)}, u32[]{:S(2)}) copy-start(f32[1,16,5120]{2,1,0:T(8,128)} %get-tuple-element.2) | copy-start | bytes 983044
  202.8 25.4 %all-to-all-start.3 = ((f32[64,16,80]{2,1,0:T(8,128)}), f32[64,16,80]{2,1,0:T(8,128)S(1)}, u32[]{:S(2)}, u32[]{:S(2)}) async-start(f32[64,16,80]{2,1,0:T(8,128)} %bitcast.31), calls=%async_computation.3 | async-start | bytes 1048576 | tf_op jit(solution)/shard_map/all_to_all | solution.py:81
  209.2 23.4 %collective-permute-start.2 = (f32[1,16,5120]{2,1,0:T(8,128)S(1)}, f32[1,16,5120]{2,1,0:T(8,128)S(1)}, u32[]{:S(2)}, u32[]{:S(2)}) collective-permute-start(f32[1,16,5120]{2,1,0:T(8,128)S(1)} %get-tuple-element.3), channel_id=1, source_target_pairs={{0,1},{1,2},{2,3},{3,4},{4,5},{5,6},{6,7},{8,9},{9,10},{10,11},{11... | collective-permute-start | bytes 983048 | tf_op jit(solution)/shard_map/ppermute | solution.py:42
  211.1 21.4 %collective-permute-start.3 = (f32[1,16,5120]{2,1,0:T(8,128)S(1)}, f32[1,16,5120]{2,1,0:T(8,128)S(1)}, u32[]{:S(2)}, u32[]{:S(2)}) collective-permute-start(f32[1,16,5120]{2,1,0:T(8,128)S(1)} %copy-done.5), channel_id=1, source_target_pairs={{1,0},{2,1},{3,2},{4,3},{5,4},{6,5},{7,6},{9,8},{10,9},{11,10},{12... | collective-permute-start | bytes 983048 | tf_op jit(solution)/shard_map/ppermute | solution.py:42
Sparse Core Ops, SparseCore 0:
  29.6 46.0 all-gather.5
  77.8 23.8 all-gather.7
where the time goes:
time: 241 us; the launch traced here: 240 us
  waiting for transfers between devices  77.5 us (32%)
  blocking collectives  52 us (22%)
  starting transfers between devices  46.2 us (19%)
  matrix products  30.6 us (13%)
  local copies, waits for them, and re-layouts  15.7 us (7%)
  between operations  14.3 us (6%)
  other arithmetic  4 us (2%)
    all_gather x2, waiting for transfers between devices, stacked_from(): parts = lax.all_gather(parts, axes[k], axis=0, tiled=True)  56.1 us
    all_to_all x1, blocking collectives, shards(): lax.all_to_all(newer[0], GRID, split_axis=1, concat_axis=0, tiled=True)  29.8 us
    all_gather x1, blocking collectives, stacked_from(): parts = lax.all_gather(parts, axes[k], axis=0, tiled=True)  22.3 us
    all_to_all x2, starting transfers between devices, shards(): lax.all_to_all(back, GRID, split_axis=0, concat_axis=1, tiled=True)[None]  18.6 us
    dot_general x2, matrix products, shards(): lax.dot_general(whole_table, spread, (((0,), (0,)), ((), ())), precision=...  17.6 us
    ppermute x4, starting transfers between devices, from_behind(): return lax.ppermute(shard, axis, pairs)  17.4 us
    all_to_all x2, waiting for transfers between devices, shards(): lax.all_to_all(back, GRID, split_axis=0, concat_axis=1, tiled=True)[None]  16.6 us
    all_to_all x1, starting transfers between devices, shards(): lax.all_to_all(newer[0], GRID, split_axis=1, concat_axis=0, tiled=True)  10 us
  transfers between devices with their start and end apart: 9, of which 6 were waited for; matrix products, arithmetic and copies ran while one was open for 12% of the time, Pallas kernels for 0%

commit v1 on v0

--- a/solution.py
+++ b/solution.py
@@ -3,6 +3,8 @@
 from jax import lax
 from jax.sharding import Mesh
 from jax.sharding import PartitionSpec as P
+from jax.experimental import pallas as pl
+from jax.experimental.pallas import tpu as pltpu
 
 RB = 80
 RS = 64
@@ -50,6 +52,49 @@
     return coef * jnp.where(offset == 0, jnp.float32(jnp.pi**2 / 3.0), 2.0 * parity / square)
 
 
+def swap_kernel(x_ref, o_ref, send_sem, recv_sem, own_sem):
+    y, z, c, h = [lax.axis_index(a) for a in GRID + ("hel",)]
+    me = (y * 4 + z) * 2 + c
+
+    def peer(d):
+        return (d // 8, lax.rem(d // 2, 4), lax.rem(d, 2), h)
+
+    barrier = pltpu.get_barrier_semaphore()
+
+    @pl.loop(1, 64)
+    def _(i):
+        pl.semaphore_signal(barrier, inc=1, device_id=peer(lax.rem(me + i, 64)), device_id_type=pl.DeviceIdType.MESH)
+
+    own = pltpu.make_async_copy(x_ref.at[me], o_ref.at[me], own_sem)
+    own.start()
+    pl.semaphore_wait(barrier, 63)
+
+    @pl.loop(1, 64)
+    def _(i):
+        d = lax.rem(me + i, 64)
+        pltpu.make_async_remote_copy(
+            src_ref=x_ref.at[d], dst_ref=o_ref.at[me], send_sem=send_sem, recv_sem=recv_sem,
+            device_id=peer(d), device_id_type=pl.DeviceIdType.MESH,
+        ).start()
+
+    own.wait()
+    pltpu.make_async_remote_copy(
+        src_ref=x_ref.at[pl.ds(0, 63)], dst_ref=o_ref.at[pl.ds(0, 63)], send_sem=send_sem, recv_sem=recv_sem,
+        device_id=peer(lax.rem(me + 1, 64)), device_id_type=pl.DeviceIdType.MESH,
+    ).wait()
+
+
+def swap(x):
+    return pl.pallas_call(
+        swap_kernel,
+        out_shape=jax.ShapeDtypeStruct(x.shape, x.dtype),
+        in_specs=[pl.BlockSpec(memory_space=pltpu.VMEM)],
+        out_specs=pl.BlockSpec(memory_space=pltpu.VMEM),
+        scratch_shapes=[pltpu.SemaphoreType.DMA, pltpu.SemaphoreType.DMA, pltpu.SemaphoreType.DMA],
+        compiler_params=pltpu.CompilerParams(collective_id=0, has_side_effects=True),
+    )(x)
+
+
 def shards(
     packet_prev,
     packet_now,
@@ -75,10 +120,10 @@
         radial = radial.reshape(newer.shape)
         below = from_behind(newer, "hel", 1)
         above = from_behind(link * newer, "hel", -1)
-        spread = lax.all_to_all(newer[0], GRID, split_axis=1, concat_axis=0, tiled=True)
+        spread = swap(newer[0].reshape(16, 64, 80).transpose(1, 0, 2)).reshape(1024, 80)
         points = lax.dot_general(whole_table, spread, (((0,), (0,)), ((), ())), precision=high)
         back = jnp.dot(whole_table, points * potential, precision=high)
-        returned = lax.all_to_all(back, GRID, split_axis=0, concat_axis=1, tiled=True)[None]
+        returned = swap(back.reshape(64, 16, 80)).transpose(1, 0, 2).reshape(1, 16, 5120)
         total = radial + rot_factor * newer + returned + link * below + above
         older, newer = (newer, 2.0 * ((total - centre * newer) / half_width) - older)
     return (older, newer)

time: 241 us -> 255 us (1.058)
  the two profiles are of different devices: /device:TPU:64 before, /device:TPU:81 now
where the time goes in v1:
time: 255 us; the launch traced here: 254 us
  Pallas kernels  104 us (41%)
  waiting for transfers between devices  47.8 us (19%)
  matrix products  29.6 us (12%)
  blocking collectives  19.5 us (8%)
  local copies, waits for them, and re-layouts  19.4 us (8%)
  starting transfers between devices  15.4 us (6%)
  between operations  14.4 us (6%)
  other arithmetic  4.02 us (2%)
    pallas_call x4, Pallas kernels, swap(): pl.pallas_call(swap_kernel, out_shape=jax.ShapeDtypeStruct(x.shape, x.dty...  104 us
    all_gather x2, waiting for transfers between devices, stacked_from(): parts = lax.all_gather(parts, axes[k], axis=0, tiled=True)  47.8 us
    all_gather x1, blocking collectives, stacked_from(): parts = lax.all_gather(parts, axes[k], axis=0, tiled=True)  19.5 us
    dot_general x2, matrix products, shards(): lax.dot_general(whole_table, spread, (((0,), (0,)), ((), ())), precision=...  15.8 us
    ppermute x4, starting transfers between devices, from_behind(): return lax.ppermute(shard, axis, pairs)  15.3 us
    dot_general x2, matrix products, shards(): back = jnp.dot(whole_table, points * potential, precision=high)  7.84 us
    another operation x4, local copies, waits for them, and re-layouts, shards(): newer[0].reshape(16, 64, 80).transpose(1, 0, 2)  5.61 us
  transfers between devices with their start and end apart: 6, of which 1 were waited for; matrix products, arithmetic and copies ran while one was open for 19% of the time, Pallas kernels for 41%

profile of v1, /device:TPU:81, one launch (start us, length us, event | category | flops | bytes accessed | tf_op | source)
XLA Modules:
  0.0 254.4 jit_solution(13263854840077775185)
XLA Ops:
  7.2 19.5 %all-gather = f32[4,1024,24]{1,2,0:T(8,128)} all-gather(f32[1,1024,24]{1,2,0:T(8,128)} %param.10), channel_id=2, replica_groups=mesh['grid_0'=8,'grid_1'=4,'grid_2'=2,'hel'=8] {'grid_1'}, dimensions={0}, use_global_device_ids=true | all-gather | bytes 491520 | tf_op jit(solution)/shard_map/all_gather | solution.py:30
  26.8 47.8 %all-gather.6.cloned.1.call-done = f32[32,1024,24]{1,2,0:T(8,128)} async-done(((f32[4,1024,24]{1,2,0:T(8,128)}), f32[32,1024,24]{1,2,0:T(8,128)}) %all-gather.6.cloned.1.call-update) | async-done | bytes 3145744 | tf_op jit(solution)/shard_map/all_gather | solution.py:30
  74.7 3.1 %collective-permute-start = (f32[1,16,5120]{2,1,0:T(8,128)}, f32[1,16,5120]{2,1,0:T(8,128)S(1)}, u32[]{:S(2)}, u32[]{:S(2)}) collective-permute-start(f32[1,16,5120]{2,1,0:T(8,128)} %param.9), channel_id=1, source_target_pairs={{0,1},{1,2},{2,3},{3,4},{4,5},{5,6},{6,7},{8,9},{9,10},{10,11},{11... | collective-permute-start | bytes 983048 | tf_op jit(solution)/shard_map/ppermute | solution.py:44
  79.6 4.3 %collective-permute-start.1 = (f32[1,16,5120]{2,1,0:T(8,128)S(1)}, f32[1,16,5120]{2,1,0:T(8,128)S(1)}, u32[]{:S(2)}, u32[]{:S(2)}) collective-permute-start(f32[1,16,5120]{2,1,0:T(8,128)S(1)} %multiply_multiply_fusion.2), channel_id=1, source_target_pairs={{1,0},{2,1},{3,2},{4,3},{5,4},{6,5},{7,6},{9,8},{10,9},{11,10},{12... | collective-permute-start | bytes 983048 | tf_op jit(solution)/shard_map/ppermute | solution.py:44
  84.0 1.2 reshape_squeeze.6
  87.5 26.8 %shard_map.101 = f32[64,16,80]{2,1,0:T(8,128)} custom-call(f32[64,16,80]{2,1,0:T(8,128)} %bitcast.86), custom_call_target="tpu_custom_call" | custom-call | tf_op jit(solution)/shard_map/pallas_call | solution.py:88
  115.1 1.7 fusion.1
  117.4 3.5 %copy.44 = f32[8,4,2,1,1024,24]{4,5,3,2,1,0:T(8,128)S(1)} copy(f32[8,4,2,1,1024,24]{4,5,3,1,0,2:T(8,128)} %bitcast.84) | data formatting | bytes 12582912 | tf_op jit(solution)/shard_map/transpose | solution.py:34
  120.9 6.3 %convolution_multiply_fusion = f32[1536,80]{0,1:T(8,128)S(1)} fusion(f32[1536,80]{0,1:T(8,128)S(1)} %copy-done.4, f32[1024,1536]{0,1:T(8,128)S(1)} %bitcast.78, f32[1024,80]{1,0:T(8,128)S(1)} %bitcast.93), kind=kOutput, calls=%fused_computation | convolution fusion | flops 1510072320 | bytes 7602176 | tf_op jit(solution)/shard_map/dot_general | solution.py:124
  127.3 3.9 %convolution_bitcast_fusion.5 = f32[1024,80]{0,1:T(8,128)S(1)} fusion(f32[1536,80]{0,1:T(8,128)S(1)} %convolution_multiply_fusion, f32[1024,1536]{0,1:T(8,128)S(1)} %bitcast.79), kind=kOutput, calls=%fused_computation.9 | convolution fusion | flops 1509949440 | bytes 7110656 | tf_op jit(solution)/shard_map/dot_general | solution.py:125
  132.2 25.6 %shard_map.102 = f32[64,16,80]{2,1,0:T(8,128)} custom-call(f32[64,16,80]{2,1,0:T(8,128)} %bitcast.87), custom_call_target="tpu_custom_call" | custom-call | tf_op jit(solution)/shard_map/pallas_call | solution.py:88
  157.8 1.2 copy.47
  161.6 1.9 collective-permute-start.2
  163.5 1.7 convolution_bitcast_fusion.1
  165.2 2.0 fusion.2
  167.2 1.4 copy.50
  169.6 2.1 copy.59
  171.7 25.8 %shard_map.103 = f32[64,16,80]{2,1,0:T(8,128)} custom-call(f32[64,16,80]{2,1,0:T(8,128)} %bitcast.89), custom_call_target="tpu_custom_call" | custom-call | tf_op jit(solution)/shard_map/pallas_call | solution.py:88
  197.6 9.4 %fusion = f32[1536,80]{0,1:T(8,128)S(1)} fusion(f32[1536,80]{0,1:T(8,128)} %param.11, f32[1024,80]{1,0:T(8,128)} %bitcast.94, f32[1024,1536]{0,1:T(8,128)} %bitcast.80), kind=kOutput, calls=%fused_computation.2 | convolution fusion | flops 1510072320 | bytes 7602176 | tf_op jit(solution)/shard_map/dot_general | solution.py:124
  207.0 6.0 %collective-permute-start.3 = (f32[1,16,5120]{2,1,0:T(8,128)}, f32[1,16,5120]{2,1,0:T(8,128)}, u32[]{:S(2)}, u32[]{:S(2)}) collective-permute-start(f32[1,16,5120]{2,1,0:T(8,128)} %get-tuple-element.2), channel_id=1, source_target_pairs={{1,0},{2,1},{3,2},{4,3},{5,4},{6,5},{7,6},{9,8},{10,9},{11,10},{12... | collective-permute-start | bytes 983048 | tf_op jit(solution)/shard_map/ppermute | solution.py:44
  213.0 3.9 %convolution_bitcast_fusion.4 = f32[1024,80]{0,1:T(8,128)S(1)} fusion(f32[1536,80]{0,1:T(8,128)S(1)} %fusion, f32[1024,1536]{0,1:T(8,128)S(1)} %bitcast.83), kind=kOutput, calls=%fused_computation.8 | convolution fusion | flops 1509949440 | bytes 7110656 | tf_op jit(solution)/shard_map/dot_general | solution.py:125
  218.0 26.1 %shard_map.104 = f32[64,16,80]{2,1,0:T(8,128)} custom-call(f32[64,16,80]{2,1,0:T(8,128)} %bitcast.90), custom_call_target="tpu_custom_call" | custom-call | tf_op jit(solution)/shard_map/pallas_call | solution.py:88
  244.1 1.2 copy.53
  245.6 2.0 fusion.16
  (53 shorter events, 11.4 us)
Async XLA Ops:
  7.2 67.5 %all-gather.6.cloned.1.call-start = ((), (), s32[]{:S(2)}) async-start(), calls=%async_computation | async-start | bytes 3538944 | tf_op jit(solution)/shard_map/all_gather | solution.py:30
  26.8 90.6 %all-gather.8.cloned.1.call-start = ((), (), s32[]{:S(2)}) async-start(), calls=%async_computation.1 | async-start | bytes 9437184 | tf_op jit(solution)/shard_map/all_gather | solution.py:30
  74.6 42.7 %copy-start.9 = (f32[64]{0:T(128)S(1)}, f32[64]{0:T(128)}, u32[]{:S(2)}) copy-start(f32[64]{0:T(128)} %param.13) | copy-start | bytes 772
  74.7 84.7 %collective-permute-start = (f32[1,16,5120]{2,1,0:T(8,128)}, f32[1,16,5120]{2,1,0:T(8,128)S(1)}, u32[]{:S(2)}, u32[]{:S(2)}) collective-permute-start(f32[1,16,5120]{2,1,0:T(8,128)} %param.9), channel_id=1, source_target_pairs={{0,1},{1,2},{2,3},{3,4},{4,5},{5,6},{6,7},{8,9},{9,10},{10,11},{11... | collective-permute-start | bytes 983048 | tf_op jit(solution)/shard_map/ppermute | solution.py:44
  79.6 79.7 %collective-permute-start.1 = (f32[1,16,5120]{2,1,0:T(8,128)S(1)}, f32[1,16,5120]{2,1,0:T(8,128)S(1)}, u32[]{:S(2)}, u32[]{:S(2)}) collective-permute-start(f32[1,16,5120]{2,1,0:T(8,128)S(1)} %multiply_multiply_fusion.2), channel_id=1, source_target_pairs={{1,0},{2,1},{3,2},{4,3},{5,4},{6,5},{7,6},{9,8},{10,9},{11,10},{12... | collective-permute-start | bytes 983048 | tf_op jit(solution)/shard_map/ppermute | solution.py:44
  117.4 3.5 %copy-start.3 = (f32[64,16,80]{2,1,0:T(8,128)S(1)}, f32[64,16,80]{2,1,0:T(8,128)}, u32[]{:S(2)}) copy-start(f32[64,16,80]{2,1,0:T(8,128)} %shard_map.101) | copy-start | bytes 983044
  117.4 3.5 %copy-start.4 = (f32[1536,80]{0,1:T(8,128)S(1)}, f32[1536,80]{0,1:T(8,128)}, u32[]{:S(2)}) copy-start(f32[1536,80]{0,1:T(8,128)} %param.11) | copy-start | bytes 1474564
  120.8 6.4 %copy-start = (f32[8,4,2,1,1024,24]{4,5,3,2,1,0:T(8,128)}, f32[8,4,2,1,1024,24]{4,5,3,2,1,0:T(8,128)S(1)}, u32[]{:S(2)}) copy-start(f32[8,4,2,1,1024,24]{4,5,3,2,1,0:T(8,128)S(1)} %copy.44) | copy-start | bytes 18874372
  127.2 32.1 %copy-start.1 = (f32[1,16,5120]{2,1,0:T(8,128)S(1)}, f32[1,16,5120]{2,1,0:T(8,128)}, u32[]{:S(2)}) copy-start(f32[1,16,5120]{2,1,0:T(8,128)} %param.9) | copy-start | bytes 983044
  127.2 32.1 %copy-start.6 = (f32[1,16,5120]{2,1,0:T(8,128)S(1)}, f32[1,16,5120]{2,1,0:T(8,128)}, u32[]{:S(2)}) copy-start(f32[1,16,5120]{2,1,0:T(8,128)} %param.8) | copy-start | bytes 983044
  127.2 32.1 %copy-start.7 = (f32[1,16]{1,0:T(1,128)S(1)}, f32[1,16]{1,0:T(1,128)}, u32[]{:S(2)}) copy-start(f32[1,16]{1,0:T(1,128)} %param.14) | copy-start | bytes 196
  127.2 32.1 %copy-start.8 = (f32[1,16]{1,0:T(1,128)S(1)}, f32[1,16]{1,0:T(1,128)}, u32[]{:S(2)}) copy-start(f32[1,16]{1,0:T(1,128)} %param.12) | copy-start | bytes 196
  160.3 85.3 %copy-start.2 = (f32[1,16,5120]{2,1,0:T(8,128)}, f32[1,16,5120]{2,1,0:T(8,128)S(1)}, u32[]{:S(2)}) copy-start(f32[1,16,5120]{2,1,0:T(8,128)S(1)} %get-tuple-element.3) | copy-start | bytes 983044
  161.6 84.0 %collective-permute-start.2 = (f32[1,16,5120]{2,1,0:T(8,128)S(1)}, f32[1,16,5120]{2,1,0:T(8,128)}, u32[]{:S(2)}, u32[]{:S(2)}) collective-permute-start(f32[1,16,5120]{2,1,0:T(8,128)S(1)} %get-tuple-element.3), channel_id=1, source_target_pairs={{0,1},{1,2},{2,3},{3,4},{4,5},{5,6},{6,7},{8,9},{9,10},{10,11},{11... | collective-permute-start | bytes 983048 | tf_op jit(solution)/shard_map/ppermute | solution.py:44
  167.2 45.8 %slice-start = ((s8[6291456]{0:T(1024)(128)(4,1)}), s8[2097152]{0:T(1024)(128)(4,1)S(1)}, s32[]{:S(2)}) async-start(s8[6291456]{0:T(1024)(128)(4,1)} %bitcast.81), calls=%async_computation.2 | async-start | bytes 4194304
  197.5 15.5 %slice-start.1 = ((s8[6291456]{0:T(1024)(128)(4,1)}), s8[4194304]{0:T(1024)(128)(4,1)S(1)}, s32[]{:S(2)}) async-start(s8[6291456]{0:T(1024)(128)(4,1)} %bitcast.81), calls=%async_computation.3 | async-start | bytes 8388608
  207.0 38.6 %copy-start.5 = (f32[1,16,5120]{2,1,0:T(8,128)S(1)}, f32[1,16,5120]{2,1,0:T(8,128)}, u32[]{:S(2)}) copy-start(f32[1,16,5120]{2,1,0:T(8,128)} %reshape.177) | copy-start | bytes 983044
  207.0 38.6 %collective-permute-start.3 = (f32[1,16,5120]{2,1,0:T(8,128)}, f32[1,16,5120]{2,1,0:T(8,128)}, u32[]{:S(2)}, u32[]{:S(2)}) collective-permute-start(f32[1,16,5120]{2,1,0:T(8,128)} %get-tuple-element.2), channel_id=1, source_target_pairs={{1,0},{2,1},{3,2},{4,3},{5,4},{6,5},{7,6},{9,8},{10,9},{11,10},{12... | collective-permute-start | bytes 983048 | tf_op jit(solution)/shard_map/ppermute | solution.py:44
Sparse Core Ops, SparseCore 0:
  26.9 47.6 all-gather.5
  76.7 25.0 all-gather.7

commit v2 on v0

v2 whole, which is shorter than its diff:
```python
import functools

import jax
import jax.numpy as jnp
import numpy as np
from jax import lax
from jax.experimental import pallas as pl
from jax.experimental.pallas import tpu as pltpu
from jax.sharding import Mesh
from jax.sharding import PartitionSpec as P

RB = 80
RS = 64
J = 1024
Q = 1536
NB = 80
ROWS = 16
TILES = 40
MSG = 10
GRID = ("grid_0", "grid_1", "grid_2")
MESH = pl.DeviceIdType.MESH

big_scale = 0.05
small_scale = 0.08
centre = 1.0
half_width = 1.5
FACTOR = 2.0 / half_width


def kinetic_entry(offset, coef):
    offset = np.asarray(offset, np.int64)
    parity = 1 - 2 * (np.abs(offset) % 2)
    square = np.maximum(offset * offset, 1)
    return (coef * np.where(offset == 0, np.pi**2 / 3.0, 2.0 * parity / square)).astype(np.float32)


def kinetic_tables():
    index = np.arange(RS)
    small = kinetic_entry(index[:, None] - index[None, :], small_scale)
    pair = np.zeros((128, 128), np.float32)
    pair[:64, :64] = small
    pair[64:, 64:] = small
    apart = 2 * (np.arange(80) - 39)
    same = np.broadcast_to(kinetic_entry(apart, big_scale)[:, None, None], (80, 8, 128))
    half = np.where(np.arange(128) < 64, -1, 1)
    other = kinetic_entry(apart[:, None] + half[None, :], big_scale)
    return pair, np.ascontiguousarray(same), np.ascontiguousarray(np.broadcast_to(other[:, None, :], (80, 8, 128)))


def lanes(shape=(8, 128)):
    return lax.broadcasted_iota(jnp.int32, shape, 1)


def turn(x, shift, axis):
    shift = shift % x.shape[axis]
    return x if shift == 0 else pltpu.roll(x, shift, axis)


def swap_blocks(x):
    row = lax.broadcasted_iota(jnp.int32, (16, 128), 0) // 2
    lane = lanes((16, 128)) // 16
    apart = (row - lane + 8) % 8
    out = x
    for delta in range(1, 8):
        moved = turn(turn(x, 2 * delta, 0), -16 * delta, 1)
        out = jnp.where(apart == delta, moved, out)
    return out


def store_message(tx, place, main, swapped, i):
    tx[place, 0:8, :] = main
    half = swapped[0:8] if i < 4 else swapped[8:16]
    tx[place, 8:16, :] = turn(half, -2 * (i % 4), 0)


def load_swapped(rx, first):
    row = lax.broadcasted_iota(jnp.int32, (8, 128), 0) // 2
    halves = []
    for top in range(2):
        out = None
        for i in range(4):
            tile = turn(rx[first + 4 * top + i, 8:16, :], 2 * i, 0)
            out = tile if out is None else jnp.where(row == i, tile, out)
        halves.append(out)
    return jnp.concatenate(halves, axis=0)


def pack_columns(src, tx, group):
    lane = lanes()
    rows = []
    for half in range(2):
        rows.append(
            [src[8 * half : 8 * half + 8, pl.ds(pl.multiple_of(group * 640 + 128 * t, 128), 128)] for t in range(5)]
        )

    def piece(tiles, start, to):
        t, o = start // 128, start % 128
        x = tiles[t]
        if o > 64:
            x = jnp.where(lane >= o, x, tiles[t + 1])
        return turn(x, to - o, 1)

    rests = []
    for half in range(2):
        out = None
        for i in range(8):
            t, o = (80 * i + 64) // 128, (80 * i + 64) % 128
            x = turn(rows[half][t], 16 * i - o, 1)
            out = x if out is None else jnp.where(lane // 16 == i, x, out)
        rests.append(out)
    swapped = swap_blocks(jnp.concatenate(rests, axis=0))
    for i in range(8):
        main = jnp.where(lane < 64, piece(rows[0], 80 * i, 0), piece(rows[1], 80 * i, 64))
        store_message(tx, group * 8 + i, main, swapped, i)


def unpack_columns(rx, group):
    lane = lanes()
    rest = swap_blocks(load_swapped(rx, group * 8))
    out = [[None] * 5, [None] * 5]
    mains = [rx[group * 8 + i, 0:8, :] for i in range(8)]
    for half in range(2):
        part = rest[8 * half : 8 * half + 8]
        for t in range(5):
            x = jnp.zeros((8, 128), jnp.float32)
            for i in range(8):
                first = 80 * i - 128 * t
                if first + 64 > 0 and first < 128:
                    moved = turn(mains[i], first - 64 * half, 1)
                    x = jnp.where((lane >= first) & (lane < first + 64), moved, x)
                first = 80 * i + 64 - 128 * t
                if first >= 0 and first < 128:
                    moved = turn(part, first - 16 * i, 1)
                    x = jnp.where((lane >= first) & (lane < first + 16), moved, x)
            out[half][t] = x
    return [jnp.concatenate([out[0][t], out[1][t]], axis=0) for t in range(5)]


def unpack_rows(rx, group):
    lane = lanes()
    rest = swap_blocks(load_swapped(rx, group * 8))
    blocks = []
    for i in range(8):
        main = rx[group * 8 + i, 0:8, :]
        for half in range(2):
            part = turn(rest[8 * half : 8 * half + 8], 64 - 16 * i, 1)
            x = jnp.where(lane < 64, turn(main, 64 * half, 1), part)
            blocks.append(jnp.where(lane < 80, x, 0.0))
    return jnp.concatenate(blocks, axis=0)


def pack_rows(x, tx, group):
    lane = lanes()
    rests = []
    for half in range(2):
        out = None
        for i in range(8):
            part = turn(x[16 * i + 8 * half : 16 * i + 8 * half + 8], 16 * i - 64, 1)
            out = part if out is None else jnp.where(lane // 16 == i, part, out)
        rests.append(out)
    swapped = swap_blocks(jnp.concatenate(rests, axis=0))
    for i in range(8):
        main = jnp.where(lane < 64, x[16 * i : 16 * i + 8], turn(x[16 * i + 8 : 16 * i + 16], 64, 1))
        store_message(tx, group * 8 + i, main, swapped, i)


def halves_of(x):
    high = x.astype(jnp.bfloat16)
    return high, (x - high.astype(jnp.float32)).astype(jnp.bfloat16)


def column(ref, m):
    return ref[:, pl.ds(pl.multiple_of(m * 128, 128), 128)]


def kernel(
    p0, p1, tt, vt, rot, rw, cpl, cent, pair, same, other,
    mid, last,
    tall, thigh, tlow, vs, pt, spread, acc, scaled, below, above, linear,
    tx0, tx1, tx2, tx3, rx0, rx1, rx2, rx3,
    own_sem, t_send, z_recv, y_recv, c_recv, a_send, a_recv, h_send, h_recv, z_ready, c_ready,
):
    txs, rxs = (tx0, tx1, tx2, tx3), (rx0, rx1, rx2, rx3)
    y, z, c, h = [lax.axis_index(a) for a in GRID + ("hel",)]

    def slot(yy, zz, cc):
        return (yy * 4 + zz) * 2 + cc

    me = slot(y, z, c)
    up, down = (lax.rem(y + 1, 8), z, c, h), (lax.rem(y + 7, 8), z, c, h)
    twin = (y, z, 1 - c, h)
    y_line = [(lax.rem(y + i, 8), z, c, h) for i in range(1, 8)]
    z_line = [(y, lax.rem(z + i, 4), c, h) for i in range(1, 4)]
    higher, lower = (y, z, c, h + 1), (y, z, c, h - 1)

    barrier = pltpu.get_barrier_semaphore()
    for device in z_line + y_line + [twin]:
        pl.semaphore_signal(barrier, inc=1, device_id=device, device_id_type=MESH)

    @pl.when(h < 7)
    def _():
        pl.semaphore_signal(barrier, inc=1, device_id=higher, device_id_type=MESH)

    @pl.when(h > 0)
    def _():
        pl.semaphore_signal(barrier, inc=1, device_id=lower, device_id_type=MESH)

    def scale(src, step):
        @pl.loop(0, TILES)
        def _(m):
            link = cpl[...] * cent[pl.ds(m, 1), :]
            scaled[step, :, pl.ds(pl.multiple_of(m * 128, 128), 128)] = link * column(src, m)

    scale(p1, 0)
    own = pltpu.make_async_copy(tt, tall.at[me], own_sem)
    own.start()

    @pl.loop(0, 8)
    def _(group):
        pack_columns(p1, tx0, group)

    lane80 = lax.broadcasted_iota(jnp.int32, (NB, 128), 1)
    for yy in range(8):
        first = 192 * yy // 128
        a, b = vt[:, 128 * first : 128 * first + 128], vt[:, 128 * first + 128 : 128 * first + 256]
        if yy % 2:
            a, b = turn(a, 64, 1), turn(b, 64, 1)
            a = jnp.where(lane80 < 64, a, b)
        vs[yy, :, 0:128] = a
        vs[yy, :, 128:256] = b

    neighbours = 11 + (h > 0).astype(jnp.int32) + (h < 7).astype(jnp.int32)
    pl.semaphore_wait(barrier, neighbours)

    def block_copy(src, dst_slot, recv, device):
        return pltpu.make_async_remote_copy(
            src_ref=src, dst_ref=tall.at[dst_slot], send_sem=t_send, recv_sem=recv, device_id=device, device_id_type=MESH
        )

    def hel_copies(step, src):
        return (
            pltpu.make_async_remote_copy(
                src_ref=src, dst_ref=below.at[step], send_sem=h_send.at[step, 0], recv_sem=h_recv.at[step, 0],
                device_id=higher, device_id_type=MESH,
            ),
            pltpu.make_async_remote_copy(
                src_ref=scaled.at[step], dst_ref=above.at[step], send_sem=h_send.at[step, 1],
                recv_sem=h_recv.at[step, 1], device_id=lower, device_id_type=MESH,
            ),
        )

    def hel_start(step, src):
        to_higher, to_lower = hel_copies(step, src)

        @pl.when(h < 7)
        def _():
            to_higher.start()

        @pl.when(h > 0)
        def _():
            to_lower.start()

    def hel_wait(step, src):
        to_higher, to_lower = hel_copies(step, src)

        @pl.when(h > 0)
        def _():
            to_higher.wait_recv()
            to_lower.wait_send()

        @pl.when(h < 7)
        def _():
            to_lower.wait_recv()
            to_higher.wait_send()

        @pl.when(h == 0)
        def _():
            below[step] = jnp.zeros((ROWS, TILES * 128), jnp.float32)

        @pl.when(h == 7)
        def _():
            above[step] = jnp.zeros((ROWS, TILES * 128), jnp.float32)

    for i in range(1, 4):
        block_copy(tt, me, z_recv.at[i - 1], z_line[i - 1]).start()
    hel_start(0, p1)
    for device in z_line:
        pl.semaphore_signal(z_ready, inc=1, device_id=device, device_id_type=MESH)

    def pass_on(dy, zz, src, ahead, behind):
        place = slot(lax.rem(y + dy + 8, 8), zz, c)
        if ahead is not None:
            block_copy(src, place, y_recv.at[0, ahead, zz], up).start()
        if behind is not None:
            block_copy(src, place, y_recv.at[1, behind, zz], down).start()
        block_copy(src, place, c_recv.at[(dy + 8) % 8, zz], twin).start()

    def arrived(recv):
        block_copy(tall.at[0], 0, recv, twin).wait_recv()

    def exchange_start(k, group, dy):
        tx, rx = txs[k], rxs[k]

        @pl.loop(0, 8)
        def _(e):
            zz, cc = lax.rem(z + e // 2, 4), lax.rem(c + lax.rem(e, 2), 2)
            to = slot(group, zz, cc)
            itself = (dy == 0) & (e == 0)

            @pl.when(jnp.logical_not(itself))
            def _():
                pltpu.make_async_remote_copy(
                    src_ref=tx.at[to, pl.ds(0, MSG)], dst_ref=rx.at[me, pl.ds(0, MSG)],
                    send_sem=a_send.at[k], recv_sem=a_recv.at[k, lax.rem(8 - dy, 8)],
                    device_id=(group, zz, cc, h), device_id_type=MESH,
                ).start()

            @pl.when(itself)
            def _():
                rx[me] = tx[me]

    def far_first(i):
        return lax.rem(jnp.where(lax.rem(i, 2) == 1, 4 - (i + 1) // 2, 4 + i // 2), 8)

    def exchange_wait(k, dy):
        tx, rx = txs[k], rxs[k]

        def wait(count):
            pltpu.make_async_remote_copy(
                src_ref=tx.at[pl.ds(0, count), pl.ds(0, MSG)], dst_ref=rx.at[pl.ds(0, count), pl.ds(0, MSG)],
                send_sem=a_send.at[k], recv_sem=a_recv.at[k, dy], device_id=twin, device_id_type=MESH,
            ).wait_recv()

        @pl.when(dy == 0)
        def _():
            wait(7)

        @pl.when(dy != 0)
        def _():
            wait(8)

    def exchange_sent(k):
        pltpu.make_async_remote_copy(
            src_ref=txs[k].at[pl.ds(0, 63), pl.ds(0, MSG)], dst_ref=rxs[k].at[pl.ds(0, 63), pl.ds(0, MSG)],
            send_sem=a_send.at[k], recv_sem=a_recv.at[k, 0], device_id=twin, device_id_type=MESH,
        ).wait_send()

    def local_part(src, older):
        turned = rot[...] * rw[...] - centre

        @pl.loop(0, TILES // 8)
        def _(g):
            def add(m, sums):
                x = column(src, m)
                parts = []
                for half in range(2):
                    xh = x[8 * half : 8 * half + 8]
                    xs = turn(xh, 64, 1)
                    for u in range(8):
                        r = 8 * g + u - m + 39
                        parts.append(sums[8 * half + u] + same[r] * xh + other[r] * xs)
                return tuple(parts)

            sums = lax.fori_loop(0, TILES, add, tuple(jnp.zeros((8, 128), jnp.float32) for _ in range(16)))
            xs = [column(src, 8 * g + u) for u in range(8)]
            small = jnp.dot(
                jnp.concatenate(xs, axis=0), pair[...],
                precision=lax.Precision.HIGHEST, preferred_element_type=jnp.float32,
            )
            for u in range(8):
                whole = jnp.concatenate([sums[u], sums[8 + u]], axis=0) + small[16 * u : 16 * u + 16]
                at = pl.ds(pl.multiple_of((8 * g + u) * 128, 128), 128)
                linear[:, at] = FACTOR * (whole + turned * xs[u]) - older[:, at]

    def add_coriolis(step):
        @pl.loop(0, TILES)
        def _(m):
            at = pl.ds(pl.multiple_of(m * 128, 128), 128)
            link = cpl[...] * cent[pl.ds(m, 1), :]
            linear[:, at] = linear[:, at] + FACTOR * (link * below[step, :, at] + above[step, :, at])

    def table_halves(yy):
        table = tall[pl.ds(yy * 8, 8)].reshape(192, J)
        high, low = halves_of(table)
        thigh[yy] = high
        tlow[yy] = low

    nt = (((1,), (1,)), ((), ()))

    def potential_part(yy, first):
        both = lax.dot_general(pt[...], thigh[yy], nt, preferred_element_type=jnp.float32)
        cross = lax.dot_general(pt[0:NB], tlow[yy], nt, preferred_element_type=jnp.float32)
        points = (both[0:NB] + both[NB:] + cross) * vs[yy, :, 0:192]
        high, low = halves_of(points)
        both = jnp.dot(jnp.concatenate([high, low], axis=0), thigh[yy], preferred_element_type=jnp.float32)
        cross = jnp.dot(high, tlow[yy], preferred_element_type=jnp.float32)
        total = both[0:NB] + both[NB:] + cross
        if first:
            acc[0:NB] = total
        else:
            acc[0:NB] = acc[0:NB] + total

    own.wait()
    pl.semaphore_wait(z_ready, 3)
    pl.semaphore_signal(c_ready, inc=1, device_id=twin, device_id_type=MESH)
    pass_on(0, z, tall.at[me], 0, 0)
    pl.semaphore_wait(c_ready, 1)

    @pl.loop(0, 8)
    def _(i):
        dy = far_first(i)
        exchange_start(0, lax.rem(y + dy, 8), dy)

    for i in range(1, 4):
        arrived(z_recv.at[i - 1])
        zz = lax.rem(z + 4 - i, 4)
        pass_on(0, zz, tall.at[slot(y, zz, c)], 0, 0)

    local_part(p1, p0)

    def ring(s):
        for zz in range(4):
            place = slot(lax.rem(y + 8 - s, 8), zz, c)
            if s < 4 or zz < 2:
                arrived(y_recv.at[0, s - 1, zz])
                pass_on(-s, zz, tall.at[place], s if s < 3 or (s == 3 and zz < 2) else None, None)
            place = slot(lax.rem(y + s, 8), zz, c)
            if s < 4 or zz >= 2:
                arrived(y_recv.at[1, s - 1, zz])
                pass_on(s, zz, tall.at[place], None, s if s < 3 or (s == 3 and zz >= 2) else None)

    def compute(dy, first=False):
        for zz in range(4):
            arrived(c_recv.at[dy % 8, zz])
        yy = lax.rem(y + dy + 8, 8)
        table_halves(yy)
        potential_part(yy, first)

    hel_wait(0, p1)
    add_coriolis(0)
    ring(1)

    @pl.loop(0, 8)
    def _(i):
        dy = far_first(i)
        group = lax.rem(y + dy, 8)
        pack_columns(linear, tx1, group)
        exchange_start(1, group, dy)

    @pl.loop(0, 8)
    def _(dy):
        exchange_wait(0, dy)
        group = lax.rem(y + dy, 8)
        at = pl.ds(pl.multiple_of(group * 128, 128), 128)
        high, low = halves_of(unpack_rows(rx0, group).T[0:NB])
        pt[0:NB, at] = high
        pt[NB : 2 * NB, at] = low

    compute(0, True)
    ring(2)
    compute(1)
    compute(-1)
    ring(3)
    compute(2)
    compute(-2)
    ring(4)

    @pl.loop(0, 8)
    def _(dy):
        exchange_wait(1, dy)
        group = lax.rem(y + dy, 8)
        at = pl.ds(pl.multiple_of(group * 128, 128), 128)
        spread[:, at] = unpack_rows(rx1, group).T[0:NB]

    compute(3)
    compute(-3)
    compute(4)

    def send_back(k):
        @pl.loop(0, 8)
        def _(i):
            dy = far_first(i)
            group = lax.rem(y + dy, 8)
            at = pl.ds(pl.multiple_of(group * 128, 128), 128)
            pack_rows(acc[:, at].T, txs[k], group)
            exchange_start(k, group, dy)

    acc[NB:128] = jnp.zeros((128 - NB, J), jnp.float32)
    send_back(2)

    @pl.loop(0, 8)
    def _(group):
        at = pl.ds(pl.multiple_of(group * 128, 128), 128)
        high, low = halves_of(spread[:, at] + FACTOR * acc[0:NB, at])
        pt[0:NB, at] = high
        pt[NB : 2 * NB, at] = low

    potential_part(0, True)

    @pl.loop(1, 8)
    def _(yy):
        potential_part(yy, False)

    send_back(3)

    def take_back(k, out):
        @pl.loop(0, 8)
        def _(dy):
            exchange_wait(k, dy)
            group = lax.rem(y + dy, 8)
            for t, tile in enumerate(unpack_columns(rxs[k], group)):
                at = pl.ds(pl.multiple_of(group * 640 + 128 * t, 128), 128)
                out[:, at] = linear[:, at] + FACTOR * tile

    take_back(2, mid)
    scale(mid, 1)
    hel_start(1, mid)
    local_part(mid, p1)
    hel_wait(1, mid)
    add_coriolis(1)
    take_back(3, last)

    for k in range(4):
        exchange_sent(k)
    pltpu.make_async_remote_copy(
        src_ref=tall.at[pl.ds(0, 63)], dst_ref=tall.at[pl.ds(0, 63)], send_sem=t_send, recv_sem=z_recv.at[0],
        device_id=twin, device_id_type=MESH,
    ).wait_send()


def shards(packet_prev, packet_now, angular_table, potential, rotation, radial_weight, coupling, centrifugal):
    pair, same, other = (jnp.asarray(a) for a in kinetic_tables())
    whole = jax.ShapeDtypeStruct((ROWS, TILES * 128), jnp.float32)
    vmem = pl.BlockSpec(memory_space=pltpu.VMEM)
    packet = (ROWS, TILES * 128)
    f32, bf16 = jnp.float32, jnp.bfloat16
    dma = pltpu.SemaphoreType.DMA
    mid, last = pl.pallas_call(
        kernel,
        out_shape=(whole, whole),
        in_specs=[vmem] * 11,
        out_specs=(vmem, vmem),
        scratch_shapes=[
            pltpu.VMEM((64, 24, J), f32),
            pltpu.VMEM((8, 192, J), bf16),
            pltpu.VMEM((8, 192, J), bf16),
            pltpu.VMEM((8, NB, 256), f32),
            pltpu.VMEM((2 * NB, J), bf16),
            pltpu.VMEM((NB, J), f32),
            pltpu.VMEM((128, J), f32),
            pltpu.VMEM((2, *packet), f32),
            pltpu.VMEM((2, *packet), f32),
            pltpu.VMEM((2, *packet), f32),
            pltpu.VMEM(packet, f32),
            *[pltpu.VMEM((64, 16, 128), f32) for _ in range(8)],
            dma,
            dma,
            dma((3,)),
            dma((2, 4, 4)),
            dma((8, 4)),
            dma((4,)),
            dma((4, 8)),
            dma((2, 2)),
            dma((2, 2)),
            pltpu.SemaphoreType.REGULAR,
            pltpu.SemaphoreType.REGULAR,
        ],
        compiler_params=pltpu.CompilerParams(collective_id=0, has_side_effects=True, vmem_limit_bytes=56 << 20),
        cost_estimate=pl.CostEstimate(flops=4 * 3 * 2 * J * Q * NB, bytes_accessed=4 << 20, transcendentals=0),
    )(
        packet_prev[0],
        packet_now[0],
        angular_table[0].T,
        potential.T,
        rotation.reshape(ROWS, 1),
        jnp.tile(radial_weight, 2).reshape(1, 128),
        coupling.reshape(ROWS, 1),
        jnp.repeat(centrifugal, RS).reshape(TILES, 128),
        pair,
        same,
        other,
    )
    return mid[None], last[None]


def solution(mesh):
    finer = Mesh(
        mesh.devices.reshape(8, 4, 2, mesh.shape["hel"]), ("grid_0", "grid_1", "grid_2", "hel")
    )
    placed = (
        P("hel", GRID, None),
        P("hel", GRID, None),
        P("hel", None, GRID),
        P(None, GRID),
        P("hel", GRID),
        P(),
        P("hel", GRID),
        P(),
    )
    return jax.shard_map(
        shards,
        mesh=finer,
        in_specs=placed,
        out_specs=(P("hel", GRID, None), P("hel", GRID, None)),
        check_vma=False,
    )
```

time: 241 us -> 136 us (0.56)
  Pallas kernels: 0 us -> 129 us
  waiting for transfers between devices: 77.5 us -> 0 us
  blocking collectives: 52 us -> 0 us
  starting transfers between devices: 46.2 us -> 0 us
  matrix products: 30.6 us -> 0 us
  between operations: 14.3 us -> 0.68 us
  local copies, waits for them, and re-layouts: 15.7 us -> 6.05 us
  other arithmetic: 4 us -> 0 us
    pallas_call x0 -> x1, Pallas kernels: none -> 129 us  [shards(): pl.pallas_call(kernel, out_shape=(whole, whole), in_specs=[vmem] * 11, ou...]
    all_gather x2 -> x0, waiting for transfers between devices: 56.1 us -> none  [stacked_from(): parts = lax.all_gather(parts, axes[k], axis=0, tiled=True)]
    dot_general x7 -> x0, matrix products: 30 us -> none  [the longest x2 17.6 us: shards(): lax.dot_general(whole_table, spread, (((0,), (0,)), ((), ())), precision=...]
    all_to_all x1 -> x0, blocking collectives: 29.8 us -> none  [shards(): lax.all_to_all(newer[0], GRID, split_axis=1, concat_axis=0, tiled=True)]
    all_to_all x3 -> x0, starting transfers between devices: 28.7 us -> none  [the longest x2 18.6 us: shards(): lax.all_to_all(back, GRID, split_axis=0, concat_axis=1, tiled=True)[None]]
    all_gather x1 -> x0, blocking collectives: 22.3 us -> none  [stacked_from(): parts = lax.all_gather(parts, axes[k], axis=0, tiled=True)]
    ppermute x4 -> x0, starting transfers between devices: 17.4 us -> none  [from_behind(): return lax.ppermute(shard, axis, pairs)]
    all_to_all x3 -> x0, waiting for transfers between devices: 16.6 us -> none  [the longest x2 16.6 us: shards(): lax.all_to_all(back, GRID, split_axis=0, concat_axis=1, tiled=True)[None]]
  transfers between devices with their start and end apart: 9 -> 0, of which waited for: 6 -> 0; matrix products, arithmetic and copies ran while one was open for 12% -> 0% of each run, Pallas kernels for 0% -> 0%
where the time goes in v2:
time: 136 us; the launch traced here: 135 us
  Pallas kernels  129 us (95%)
  local copies, waits for them, and re-layouts  6.05 us (4%)
    pallas_call x1, Pallas kernels, shards(): pl.pallas_call(kernel, out_shape=(whole, whole), in_specs=[vmem] * 11, ou...  129 us
    unnamed x12, local copies, waits for them, and re-layouts  3.24 us

profile of v2, /device:TPU:64, one launch (start us, length us, event | category | flops | bytes accessed | tf_op | source)
XLA Modules:
  0.0 135.3 jit_solution(6210554202789579637)
XLA Ops:
  0.6 0.0 copy-start.4
  0.6 0.6 copy-done.4
  1.3 0.0 copy-start.1
  1.3 0.6 reshape_tile.3.rw
  1.9 0.1 copy-done.1
  1.9 0.0 copy-start.2
  1.9 0.7 copy.15.rot
  2.6 0.0 copy-done.2
  2.6 0.0 copy-start.3
  2.6 0.7 copy.16.cpl
  3.3 0.0 copy-done.3
  3.3 0.1 broadcast_in_dim.13
  3.4 0.1 broadcast_in_dim.14
  3.5 0.7 broadcast_in_dim.15.cent
  4.2 128.6 %shard_map.122 = (f32[16,5120]{1,0:T(8,128)}, f32[16,5120]{1,0:T(8,128)}) custom-call(f32[16,5120]{1,0:T(8,128)} %bitcast.15, f32[16,5120]{1,0:T(8,128)} %bitcast.16, f32[24,1024]{1,0:T(8,128)} %bitcast.17, f32[80,1536]{1,0:T(8,128)} %bitcast.14, f32[16,1]{1,0:T(8,128)} %copy.15.rot, f32[1,128]{1,0:T(1,128)} %reshape_tile.3.rw, f32[16,1]{1,0:T(8,128)} %copy.16.cpl, ...), custom_call_target="tpu_custom_call" | custom-call | flops 3019898880 | bytes 4194304 | tf_op jit(solution)/shard_map/pallas_call | solution.py:538
  132.8 0.0 copy-start
  132.8 1.8 %copy.19 = f32[1,16,5120]{2,1,0:T(8,128)} copy(f32[1,16,5120]{2,1,0:T(8,128)} %bitcast.11) | data formatting | bytes 655360
  134.6 0.0 copy-done
  134.6 0.7 copy.20
  (1 shorter events, 0.0 us)
Async XLA Ops:
  0.6 0.7 copy-start.4
  1.3 0.7 copy-start.1
  1.9 0.7 copy-start.2
  2.6 0.7 copy-start.3
  132.8 1.8 %copy-start = (f32[16,5120]{1,0:T(8,128)S(1)}, f32[16,5120]{1,0:T(8,128)}, u32[]{:S(2)}) copy-start(f32[16,5120]{1,0:T(8,128)} %get-tuple-element.5) | copy-start | bytes 983044

commit v3 on v2

v3 whole, which is shorter than its diff:
```python
import functools

import jax
import jax.numpy as jnp
import numpy as np
from jax import lax
from jax.experimental import pallas as pl
from jax.experimental.pallas import tpu as pltpu
from jax.sharding import Mesh
from jax.sharding import PartitionSpec as P

RB = 80
RS = 64
J = 1024
Q = 1536
NB = 80
ROWS = 16
TILES = 40
MSG = 10
GRID = ("grid_0", "grid_1", "grid_2")
MESH = pl.DeviceIdType.MESH

big_scale = 0.05
small_scale = 0.08
centre = 1.0
half_width = 1.5
FACTOR = 2.0 / half_width


def kinetic_entry(offset, coef):
    offset = np.asarray(offset, np.int64)
    parity = 1 - 2 * (np.abs(offset) % 2)
    square = np.maximum(offset * offset, 1)
    return (coef * np.where(offset == 0, np.pi**2 / 3.0, 2.0 * parity / square)).astype(np.float32)


def two_halves(x):
    high = x.astype(jnp.bfloat16)
    return high, (x - high.astype(np.float32)).astype(jnp.bfloat16)


def kinetic_tables():
    index = np.arange(RS)
    pair = np.zeros((128, 128), np.float32)
    pair[:64, :64] = pair[64:, 64:] = kinetic_entry(index[:, None] - index[None, :], small_scale)
    high, low = two_halves(pair)
    small = np.concatenate([high, high, low], axis=0)
    apart = 2 * (np.arange(TILES)[:, None] - np.arange(TILES)[None, :])
    big = np.zeros((128, 48), np.float32)
    for i, more in enumerate((0, -1, 1)):
        big[40 * i : 40 * i + 40, :40] = kinetic_entry(apart + more, big_scale)
    high, low = two_halves(big)
    return small, np.concatenate([high, high, low], axis=1)


def lanes(shape=(8, 128)):
    return lax.broadcasted_iota(jnp.int32, shape, 1)


def turn(x, shift, axis):
    shift = shift % x.shape[axis]
    return x if shift == 0 else pltpu.roll(x, shift, axis)


def swap_blocks(x):
    row = lax.broadcasted_iota(jnp.int32, (16, 128), 0) // 2
    lane = lanes((16, 128)) // 16
    apart = (row - lane + 8) % 8
    out = x
    for delta in range(1, 8):
        moved = turn(turn(x, 2 * delta, 0), -16 * delta, 1)
        out = jnp.where(apart == delta, moved, out)
    return out


def store_message(tx, place, main, swapped, i):
    tx[place, 0:8, :] = main
    half = swapped[0:8] if i < 4 else swapped[8:16]
    tx[place, 8:16, :] = turn(half, -2 * (i % 4), 0)


def load_swapped(rx, first):
    row = lax.broadcasted_iota(jnp.int32, (8, 128), 0) // 2
    halves = []
    for top in range(2):
        out = None
        for i in range(4):
            tile = turn(rx[first + 4 * top + i, 8:16, :], 2 * i, 0)
            out = tile if out is None else jnp.where(row == i, tile, out)
        halves.append(out)
    return jnp.concatenate(halves, axis=0)


def pack_columns(src, tx, group, extra=None):
    lane = lanes()
    rows = []
    for half in range(2):
        rows.append(
            [src[8 * half : 8 * half + 8, pl.ds(pl.multiple_of(group * 640 + 128 * t, 128), 128)] for t in range(5)]
        )

    def piece(tiles, start, to):
        t, o = start // 128, start % 128
        x = tiles[t]
        if o > 64:
            x = jnp.where(lane >= o, x, tiles[t + 1])
        return turn(x, to - o, 1)

    rests = []
    for half in range(2):
        out = None
        for i in range(8):
            t, o = (80 * i + 64) // 128, (80 * i + 64) % 128
            x = turn(rows[half][t], 16 * i - o, 1)
            out = x if out is None else jnp.where(lane // 16 == i, x, out)
        rests.append(out)
    swapped = swap_blocks(jnp.concatenate(rests, axis=0))
    for i in range(8):
        main = jnp.where(lane < 64, piece(rows[0], 80 * i, 0), piece(rows[1], 80 * i, 64))
        store_message(tx, group * 8 + i, main, swapped, i)
        if extra is not None:
            tx[group * 8 + i, MSG : MSG + 1, 0:ROWS] = extra[...]


def unpack_columns(rx, group):
    lane = lanes()
    rest = swap_blocks(load_swapped(rx, group * 8))
    out = [[None] * 5, [None] * 5]
    mains = [rx[group * 8 + i, 0:8, :] for i in range(8)]
    for half in range(2):
        part = rest[8 * half : 8 * half + 8]
        for t in range(5):
            x = jnp.zeros((8, 128), jnp.float32)
            for i in range(8):
                first = 80 * i - 128 * t
                if first + 64 > 0 and first < 128:
                    moved = turn(mains[i], first - 64 * half, 1)
                    x = jnp.where((lane >= first) & (lane < first + 64), moved, x)
                first = 80 * i + 64 - 128 * t
                if first >= 0 and first < 128:
                    moved = turn(part, first - 16 * i, 1)
                    x = jnp.where((lane >= first) & (lane < first + 16), moved, x)
            out[half][t] = x
    return [jnp.concatenate([out[0][t], out[1][t]], axis=0) for t in range(5)]


def unpack_rows(rx, group):
    lane = lanes()
    rest = swap_blocks(load_swapped(rx, group * 8))
    blocks = []
    for i in range(8):
        main = rx[group * 8 + i, 0:8, :]
        for half in range(2):
            part = turn(rest[8 * half : 8 * half + 8], 64 - 16 * i, 1)
            x = jnp.where(lane < 64, turn(main, 64 * half, 1), part)
            blocks.append(jnp.where(lane < 80, x, 0.0))
    return jnp.concatenate(blocks, axis=0)


def pack_rows(x, tx, group):
    lane = lanes()
    rests = []
    for half in range(2):
        out = None
        for i in range(8):
            part = turn(x[16 * i + 8 * half : 16 * i + 8 * half + 8], 16 * i - 64, 1)
            out = part if out is None else jnp.where(lane // 16 == i, part, out)
        rests.append(out)
    swapped = swap_blocks(jnp.concatenate(rests, axis=0))
    for i in range(8):
        main = jnp.where(lane < 64, x[16 * i : 16 * i + 8], turn(x[16 * i + 8 : 16 * i + 16], 64, 1))
        store_message(tx, group * 8 + i, main, swapped, i)


def halves_of(x):
    high = x.astype(jnp.bfloat16)
    return high, (x - high.astype(jnp.float32)).astype(jnp.bfloat16)


def column(ref, m):
    return ref[:, pl.ds(pl.multiple_of(m * 128, 128), 128)]


def kernel(
    p0, p1, tt, vt, rot, rw, cpl, cent, small_op, big_op,
    mid, last,
    tall, thigh, tlow, vs, pt, weighted, spread, acc, scaled, below, above, linear, link, stacked, radial, turned, couplings,
    scaled_points, below_points, above_points,
    tx0, tx1, tx2, tx3, rx0, rx1, rx2, rx3,
    own_sem, t_send, z_recv, y_recv, c_recv,
    a_send, a_recv, h_send, h_recv, g_send, g_recv, z_ready, c_ready,
):
    txs, rxs = (tx0, tx1, tx2, tx3), (rx0, rx1, rx2, rx3)
    y, z, c, h = [lax.axis_index(a) for a in GRID + ("hel",)]

    def slot(yy, zz, cc):
        return (yy * 4 + zz) * 2 + cc

    me = slot(y, z, c)
    up, down = (lax.rem(y + 1, 8), z, c, h), (lax.rem(y + 7, 8), z, c, h)
    twin = (y, z, 1 - c, h)
    y_line = [(lax.rem(y + i, 8), z, c, h) for i in range(1, 8)]
    z_line = [(y, lax.rem(z + i, 4), c, h) for i in range(1, 4)]
    higher, lower = (y, z, c, h + 1), (y, z, c, h - 1)

    barrier = pltpu.get_barrier_semaphore()
    for device in z_line + y_line + [twin]:
        pl.semaphore_signal(barrier, inc=1, device_id=device, device_id_type=MESH)

    @pl.when(h < 7)
    def _():
        pl.semaphore_signal(barrier, inc=1, device_id=higher, device_id_type=MESH)

    @pl.when(h > 0)
    def _():
        pl.semaphore_signal(barrier, inc=1, device_id=lower, device_id_type=MESH)

    own = pltpu.make_async_copy(tt, tall.at[me], own_sem)
    own.start()
    neighbours = 11 + (h > 0).astype(jnp.int32) + (h < 7).astype(jnp.int32)
    pl.semaphore_wait(barrier, neighbours)

    def hel_copies(up_src, up_dst, down_src, down_dst, send, recv):
        return (
            pltpu.make_async_remote_copy(
                src_ref=up_src, dst_ref=up_dst, send_sem=send(0), recv_sem=recv(0), device_id=higher, device_id_type=MESH
            ),
            pltpu.make_async_remote_copy(
                src_ref=down_src, dst_ref=down_dst, send_sem=send(1), recv_sem=recv(1), device_id=lower, device_id_type=MESH
            ),
        )

    def hel_first():
        return hel_copies(p1, below, scaled, above, lambda i: h_send.at[i], lambda i: h_recv.at[i])

    def hel_second(i, at):
        return hel_copies(
            spread.at[:, at], below_points.at[:, at], scaled_points.at[:, at], above_points.at[:, at],
            lambda way: g_send.at[i, way], lambda way: g_recv.at[i, way],
        )

    def hel_start(copies, ways=(0, 1)):
        if 0 in ways:

            @pl.when(h < 7)
            def _():
                copies()[0].start()

        if 1 in ways:

            @pl.when(h > 0)
            def _():
                copies()[1].start()

    def hel_wait(copies):
        @pl.when(h > 0)
        def _():
            copies()[0].wait_recv()

        @pl.when(h > 0)
        def _():
            copies()[1].wait_send()

        @pl.when(h < 7)
        def _():
            copies()[1].wait_recv()

        @pl.when(h < 7)
        def _():
            copies()[0].wait_send()

    def table_copy(place, part, recv, device, src=None):
        return pltpu.make_async_remote_copy(
            src_ref=(tall.at[place] if src is None else src).at[part], dst_ref=tall.at[place].at[part],
            send_sem=t_send, recv_sem=recv, device_id=device, device_id_type=MESH,
        )

    def arrived(recv, part):
        table_copy(0, part, recv, twin).wait_recv()

    REST = pl.ds(0, 24)

    def at_y(dy):
        return lax.rem(y + 8 + dy, 8)

    def rest_on(dy, zz, ahead, behind, src=None):
        place = slot(at_y(dy), zz, c)
        if ahead is not None:
            table_copy(place, REST, y_recv.at[0, ahead, zz], up, src).start()
        if behind is not None:
            table_copy(place, REST, y_recv.at[1, behind, zz], down, src).start()
        table_copy(place, REST, c_recv.at[dy % 8, zz], twin, src).start()

    def ring_rest(s):
        for i in range(4):
            zz = lax.rem(z + 4 - i, 4)
            on = s < 3 or (s == 3 and i < 2)
            if s < 4 or i < 2:
                arrived(y_recv.at[0, s - 1, zz], REST)
                rest_on(-s, zz, s if on else None, None)
            on = s < 3 or (s == 3 and i >= 2)
            if s < 4 or i >= 2:
                arrived(y_recv.at[1, s - 1, zz], REST)
                rest_on(s, zz, None, s if on else None)

    for i in range(1, 4):
        table_copy(me, REST, z_recv.at[i - 1], z_line[i - 1], tt).start()
    rest_on(0, z, 0, 0, tt)
    hel_start(hel_first, (0,))
    for device in z_line:
        pl.semaphore_signal(z_ready, inc=1, device_id=device, device_id_type=MESH)

    @pl.when(h == 0)
    def _():
        below[...] = jnp.zeros_like(below)
        below_points[...] = jnp.zeros_like(below_points)

    @pl.when(h == 7)
    def _():
        above[...] = jnp.zeros_like(above)
        above_points[...] = jnp.zeros_like(above_points)

    def exchange_start(k, group, dy):
        tx, rx = txs[k], rxs[k]
        rows = MSG + 1 if k == 0 else MSG

        @pl.loop(0, 8)
        def _(e):
            zz, cc = lax.rem(z + e // 2, 4), lax.rem(c + lax.rem(e, 2), 2)
            to = slot(group, zz, cc)
            itself = (dy == 0) & (e == 0)

            @pl.when(jnp.logical_not(itself))
            def _():
                pltpu.make_async_remote_copy(
                    src_ref=tx.at[to, pl.ds(0, rows)], dst_ref=rx.at[me, pl.ds(0, rows)],
                    send_sem=a_send.at[k], recv_sem=a_recv.at[k, lax.rem(8 - dy, 8)],
                    device_id=(group, zz, cc, h), device_id_type=MESH,
                ).start()

            @pl.when(itself)
            def _():
                rx[me] = tx[me]

    def far_first(i):
        return lax.rem(jnp.where(lax.rem(i, 2) == 1, 4 - (i + 1) // 2, 4 + i // 2), 8)

    def exchange_wait(k, dy):
        tx, rx = txs[k], rxs[k]
        rows = MSG + 1 if k == 0 else MSG

        def wait(count):
            pltpu.make_async_remote_copy(
                src_ref=tx.at[pl.ds(0, count), pl.ds(0, rows)], dst_ref=rx.at[pl.ds(0, count), pl.ds(0, rows)],
                send_sem=a_send.at[k], recv_sem=a_recv.at[k, dy], device_id=twin, device_id_type=MESH,
            ).wait_recv()

        @pl.when(dy == 0)
        def _():
            wait(7)

        @pl.when(dy != 0)
        def _():
            wait(8)

    def exchange_sent(k):
        rows = MSG + 1 if k == 0 else MSG
        pltpu.make_async_remote_copy(
            src_ref=txs[k].at[pl.ds(0, 63), pl.ds(0, rows)], dst_ref=rxs[k].at[pl.ds(0, 63), pl.ds(0, rows)],
            send_sem=a_send.at[k], recv_sem=a_recv.at[k, 0], device_id=twin, device_id_type=MESH,
        ).wait_send()

    def radial_big(src):
        for m in range(TILES):
            stacked[16 * m : 16 * m + 16] = src[:, 128 * m : 128 * m + 128]
        left = lanes((TILES, 128)) < 64

        @pl.loop(0, 2)
        def _(q):
            for r in range(4):
                j = 8 * q + 2 * r
                rows = [stacked[pl.ds(j + k, 48, stride=16), :] for k in range(2)]
                high, low = halves_of(jnp.concatenate(rows, axis=1))
                data = jnp.concatenate([high, low, high], axis=0)
                result = jnp.dot(big_op[...], data, preferred_element_type=jnp.float32)
                for k in range(2):
                    part = result[:, 128 * k : 128 * k + 128]
                    crossed = jnp.where(left, part[80:120], part[40:80])
                    radial[pl.ds(j + k, TILES, stride=16), :] = part[0:40] + turn(crossed, 64, 1)

    def local_part(src, older):
        @pl.loop(0, TILES // 8)
        def _(g):
            rows = stacked[pl.ds(pl.multiple_of(128 * g, 128), 128), :]
            high, low = halves_of(rows)
            small = jnp.dot(
                jnp.concatenate([high, low, high], axis=1), small_op[...], preferred_element_type=jnp.float32
            )
            whole = small + radial[pl.ds(pl.multiple_of(128 * g, 128), 128), :]
            for u in range(8):
                at = pl.ds(pl.multiple_of((8 * g + u) * 128, 128), 128)
                block = slice(16 * u, 16 * u + 16)
                linear[:, at] = FACTOR * (whole[block] + turned[...] * rows[block]) - older[:, at]

    def by_tiles(body):
        @pl.loop(0, TILES // 8)
        def _(g):
            for u in range(8):
                body(8 * g + u, pl.ds(pl.multiple_of((8 * g + u) * 128, 128), 128))

    def add_coriolis():
        def body(m, at):
            linear[:, at] = linear[:, at] + FACTOR * (link[:, at] * below[:, at] + above[:, at])

        by_tiles(body)

    def table_halves(yy):
        table = tall[pl.ds(yy * 8, 8)].reshape(192, J)
        high, low = halves_of(table)
        at = pl.ds(pl.multiple_of(yy * 192, 64), 192)
        thigh[at] = high
        tlow[at] = low

    nt = (((1,), (1,)), ((), ()))

    def points_of(at, potential):
        both = lax.dot_general(pt[...], thigh[at], nt, preferred_element_type=jnp.float32)
        cross = lax.dot_general(pt[0:NB], tlow[at], nt, preferred_element_type=jnp.float32)
        high, low = halves_of((both[0:NB] + both[NB:] + cross) * potential)
        return jnp.concatenate([high, low], axis=0)

    def back_of(points, high, low):
        both = jnp.dot(points, high, preferred_element_type=jnp.float32)
        cross = jnp.dot(points[0:NB], low, preferred_element_type=jnp.float32)
        return both[0:NB] + both[NB:] + cross

    def potential_part(yy, first):
        at = pl.ds(pl.multiple_of(yy * 192, 64), 192)
        total = back_of(points_of(at, vs[yy, :, 0:192]), thigh[at], tlow[at])
        if first:
            acc[0:NB] = total
        else:
            acc[0:NB] = acc[0:NB] + total

    diagonal = lax.broadcasted_iota(jnp.int32, (ROWS, ROWS), 0) == lanes((ROWS, ROWS))
    of_rows = lambda ref: jnp.sum(jnp.where(diagonal, ref[...], 0.0), axis=1, keepdims=True)
    lane = lanes((1, 128))
    centrifugal = cent[...]

    def pick(at):
        return jnp.sum(jnp.where(at == lanes((at.shape[0], RB)), centrifugal, 0.0), axis=1, keepdims=True)

    tile_at = lax.broadcasted_iota(jnp.int32, (TILES, 1), 0)
    of_tiles = jnp.where(lanes((TILES, 128)) < 64, pick(2 * tile_at), pick(2 * tile_at + 1))
    own_coupling = jnp.broadcast_to(of_rows(cpl), (ROWS, 128))
    for m in range(TILES):
        at = slice(128 * m, 128 * m + 128)
        factor = own_coupling * of_tiles[m : m + 1]
        link[:, at] = factor
        scaled[:, at] = factor * p1[:, at]
    hel_start(hel_first, (1,))

    @pl.loop(0, 8)
    def _(group):
        pack_columns(p1, tx0, group, cpl)


    pl.semaphore_wait(z_ready, 3)
    pl.semaphore_signal(c_ready, inc=1, device_id=twin, device_id_type=MESH)
    pl.semaphore_wait(c_ready, 1)

    @pl.loop(0, 8)
    def _(i):
        dy = far_first(i)
        exchange_start(0, lax.rem(y + dy, 8), dy)

    for i in range(1, 4):
        arrived(z_recv.at[i - 1], REST)
        rest_on(0, lax.rem(z + 4 - i, 4), 0, 0)

    weight = jnp.concatenate([rw[...], rw[...]], axis=1)
    turned[...] = of_rows(rot) * weight - centre
    stacked[640:768] = jnp.zeros((128, 128), jnp.float32)
    radial_big(p1)
    local_part(p1, p0)
    ring_rest(1)

    lane80 = lax.broadcasted_iota(jnp.int32, (NB, 128), 1)
    for yy in range(8):
        first = 192 * yy // 128
        a, b = vt[:, 128 * first : 128 * first + 128], vt[:, 128 * first + 128 : 128 * first + 256]
        if yy % 2:
            a, b = turn(a, 64, 1), turn(b, 64, 1)
            a = jnp.where(lane80 < 64, a, b)
        vs[yy, :, 0:128] = a
        vs[yy, :, 128:256] = b

    def compute(dy, first=False):
        for zz in range(4):
            arrived(c_recv.at[dy % 8, zz], REST)
        yy = at_y(dy)
        table_halves(yy)
        potential_part(yy, first)

    hel_wait(hel_first)
    add_coriolis()

    @pl.loop(0, 8)
    def _(i):
        dy = far_first(i)
        group = lax.rem(y + dy, 8)
        pack_columns(linear, tx1, group)
        exchange_start(1, group, dy)

    ring_rest(2)

    @pl.loop(0, 8)
    def _(dy):
        exchange_wait(0, dy)
        group = lax.rem(y + dy, 8)
        at = pl.ds(pl.multiple_of(group * 128, 128), 128)
        high, low = halves_of(unpack_rows(rx0, group).T[0:NB])
        pt[0:NB, at] = high
        pt[NB : 2 * NB, at] = low
        row = jnp.zeros((1, 128), jnp.float32)
        for i in range(8):
            part = turn(rx0[group * 8 + i, 8:16, :], 16 * i, 1)[2:3]
            row = jnp.where(lane // 16 == i, part, row)
        couplings[:, at] = row

    own.wait()
    compute(0, True)
    compute(1)
    compute(-1)
    ring_rest(3)
    compute(2)
    compute(-2)
    ring_rest(4)

    @pl.loop(0, 8)
    def _(dy):
        exchange_wait(1, dy)
        group = lax.rem(y + dy, 8)
        at = pl.ds(pl.multiple_of(group * 128, 128), 128)
        spread[:, at] = unpack_rows(rx1, group).T[0:NB]

    compute(3)
    compute(-3)
    compute(4)

    acc[NB:128] = jnp.zeros((128 - NB, J), jnp.float32)
    own_centrifugal = pick((me * NB + lax.broadcasted_iota(jnp.int32, (NB, 1), 0)) // RS)

    def pair_of(i):
        return lax.rem(y // 2 + jnp.where(i == 0, 2, jnp.where(i == 3, 0, 2 * i - 1)), 4)

    @pl.loop(0, 4)
    def _(i):
        at = pl.ds(pl.multiple_of(pair_of(i) * 256, 256), 256)
        packet = spread[:, at] + FACTOR * acc[0:NB, at]
        spread[:, at] = packet
        scaled_points[:, at] = own_centrifugal * couplings[:, at] * packet
        hel_start(lambda: hel_second(i, at))
        high, low = halves_of(packet)
        pt[0:NB, at] = high
        pt[NB : 2 * NB, at] = low

    @pl.loop(0, 8)
    def _(i):
        dy = far_first(i)
        group = lax.rem(y + dy, 8)
        pack_rows(acc[:, pl.ds(pl.multiple_of(group * 128, 128), 128)].T, tx2, group)
        exchange_start(2, group, dy)

    @pl.loop(0, 6)
    def _(i):
        at = pl.ds(pl.multiple_of(i * 256, 256), 256)
        weighted[:, at] = points_of(at, vt[:, at])

    @pl.loop(0, 4)
    def _(i):
        pair_at = pair_of(i)
        at = pl.ds(pl.multiple_of(pair_at * 256, 256), 256)
        total = back_of(weighted[...], thigh[:, at], tlow[:, at])
        hel_wait(lambda: hel_second(i, at))
        factor = own_centrifugal * couplings[:, at]
        acc[0:NB, at] = total + (factor * below_points[:, at] + above_points[:, at])
        for part in range(2):
            group = 2 * pair_at + part
            pack_rows(acc[:, pl.ds(pl.multiple_of(group * 128, 128), 128)].T, tx3, group)
            exchange_start(3, group, lax.rem(group - y + 8, 8))

    def take_back(k, out):
        @pl.loop(0, 8)
        def _(dy):
            exchange_wait(k, dy)
            group = lax.rem(y + dy, 8)
            for t, tile in enumerate(unpack_columns(rxs[k], group)):
                at = pl.ds(pl.multiple_of(group * 640 + 128 * t, 128), 128)
                out[:, at] = linear[:, at] + FACTOR * tile

    take_back(2, mid)
    radial_big(mid)
    local_part(mid, p1)
    take_back(3, last)

    for k in range(4):
        exchange_sent(k)
    pltpu.make_async_remote_copy(
        src_ref=tall.at[pl.ds(0, 63)], dst_ref=tall.at[pl.ds(0, 63)], send_sem=t_send, recv_sem=z_recv.at[0],
        device_id=twin, device_id_type=MESH,
    ).wait_send()


def hand_out(mid, last, mid_out, last_out):
    mid_out[...] = mid[...]
    last_out[...] = last[...]


def shards(packet_prev, packet_now, angular_table, potential, rotation, radial_weight, coupling, centrifugal):
    small_op, big_op = (jnp.asarray(a) for a in kinetic_tables())
    whole = jax.ShapeDtypeStruct((ROWS, TILES * 128), jnp.float32)
    vmem = pl.BlockSpec(memory_space=pltpu.VMEM)
    packet = (ROWS, TILES * 128)
    f32, bf16 = jnp.float32, jnp.bfloat16
    dma = pltpu.SemaphoreType.DMA
    mid, last = pl.pallas_call(
        kernel,
        out_shape=(whole, whole),
        in_specs=[vmem] * 10,
        out_specs=(vmem, vmem),
        scratch_shapes=[
            pltpu.VMEM((64, 24, J), f32),
            pltpu.VMEM((Q, J), bf16),
            pltpu.VMEM((Q, J), bf16),
            pltpu.VMEM((8, NB, 256), f32),
            pltpu.VMEM((2 * NB, J), bf16),
            pltpu.VMEM((2 * NB, Q), bf16),
            pltpu.VMEM((NB, J), f32),
            pltpu.VMEM((128, J), f32),
            *[pltpu.VMEM(packet, f32) for _ in range(5)],
            pltpu.VMEM((768, 128), f32),
            pltpu.VMEM((640, 128), f32),
            pltpu.VMEM((ROWS, 128), f32),
            pltpu.VMEM((1, J), f32),
            *[pltpu.VMEM((NB, J), f32) for _ in range(3)],
            *[pltpu.VMEM((64, 16, 128), f32) for _ in range(8)],
            dma,
            dma,
            dma((3,)),
            dma((2, 4, 4)),
            dma((8, 4)),
            dma((4,)),
            dma((4, 8)),
            dma((2,)),
            dma((2,)),
            dma((4, 2)),
            dma((4, 2)),
            pltpu.SemaphoreType.REGULAR,
            pltpu.SemaphoreType.REGULAR,
        ],
        compiler_params=pltpu.CompilerParams(collective_id=0, has_side_effects=True, vmem_limit_bytes=56 << 20),
        cost_estimate=pl.CostEstimate(flops=4 * 3 * 2 * J * Q * NB, bytes_accessed=4 << 20, transcendentals=0),
    )(
        packet_prev[0],
        packet_now[0],
        angular_table[0].T,
        potential.T,
        rotation,
        radial_weight.reshape(1, RS),
        coupling,
        centrifugal.reshape(1, RB),
        small_op,
        big_op,
    )
    mid, last = pl.pallas_call(
        hand_out, out_shape=(whole, whole), in_specs=[vmem] * 2, out_specs=(vmem, vmem)
    )(mid, last)
    return mid[None], last[None]


def solution(mesh):
    finer = Mesh(
        mesh.devices.reshape(8, 4, 2, mesh.shape["hel"]), ("grid_0", "grid_1", "grid_2", "hel")
    )
    placed = (
        P("hel", GRID, None),
        P("hel", GRID, None),
        P("hel", None, GRID),
        P(None, GRID),
        P("hel", GRID),
        P(),
        P("hel", GRID),
        P(),
    )
    return jax.shard_map(
        shards,
        mesh=finer,
        in_specs=placed,
        out_specs=(P("hel", GRID, None), P("hel", GRID, None)),
        check_vma=False,
    )
```

time: 136 us -> 105 us (0.77)
  the two profiles are of different devices: /device:TPU:64 before, /device:TPU:15 now
where the time goes in v3:
time: 105 us
  Pallas kernels  104 us (99%)
    pallas_call x1, Pallas kernels, shards(): pl.pallas_call(kernel, out_shape=(whole, whole), in_specs=[vmem] * 10, ou...  102 us

profile of v3, /device:TPU:15, one launch (start us, length us, event | category | flops | bytes accessed | tf_op | source)
XLA Modules:
  0.0 104.7 jit_solution(12988052512107027858)
XLA Ops:
  0.6 102.1 %shard_map.113 = (f32[16,5120]{1,0:T(8,128)}, f32[16,5120]{1,0:T(8,128)}) custom-call(f32[16,5120]{1,0:T(8,128)} %bitcast.11, f32[16,5120]{1,0:T(8,128)} %bitcast.12, f32[24,1024]{1,0:T(8,128)} %bitcast.15, f32[80,1536]{1,0:T(8,128)} %bitcast.10, f32[1,16]{1,0:T(1,128)} %rot.1, f32[1,64]{1,0:T(1,128)} %bitcast.16, f32[1,16]{1,0:T(1,128)} %cpl.1, ...), custom_call_target="tpu_custom_call" | custom-call | flops 3019898880 | bytes 4194304 | tf_op jit(solution)/shard_map/pallas_call | solution.py:627
  102.8 1.9 %shard_map.114 = (f32[16,5120]{1,0:T(8,128)}, f32[16,5120]{1,0:T(8,128)}) custom-call(f32[16,5120]{1,0:T(8,128)} %get-tuple-element.6.mid, f32[16,5120]{1,0:T(8,128)} %get-tuple-element.7.last), custom_call_target="tpu_custom_call" | custom-call | tf_op jit(solution)/shard_map/pallas_call | solution.py:676

commit v4 on v3

--- a/solution.py
+++ b/solution.py
@@ -292,8 +292,8 @@
         table_copy(place, REST, c_recv.at[dy % 8, zz], twin, src).start()
 
     def ring_rest(s):
-        for i in range(4):
-            zz = lax.rem(z + 4 - i, 4)
+        for i, far in enumerate((0, 1, 3, 2)):
+            zz = lax.rem(z + 4 - far, 4)
             on = s < 3 or (s == 3 and i < 2)
             if s < 4 or i < 2:
                 arrived(y_recv.at[0, s - 1, zz], REST)
@@ -303,7 +303,7 @@
                 arrived(y_recv.at[1, s - 1, zz], REST)
                 rest_on(s, zz, None, s if on else None)
 
-    for i in range(1, 4):
+    for i in (1, 3, 2):
         table_copy(me, REST, z_recv.at[i - 1], z_line[i - 1], tt).start()
     rest_on(0, z, 0, 0, tt)
     hel_start(hel_first, (0,))
@@ -324,23 +324,25 @@
         tx, rx = txs[k], rxs[k]
         rows = MSG + 1 if k == 0 else MSG
 
-        @pl.loop(0, 8)
-        def _(e):
-            zz, cc = lax.rem(z + e // 2, 4), lax.rem(c + lax.rem(e, 2), 2)
+        def send(e):
+            zz, cc = lax.rem(z + e // 2, 4), (1 - c if e % 2 else c)
             to = slot(group, zz, cc)
-            itself = (dy == 0) & (e == 0)
-
-            @pl.when(jnp.logical_not(itself))
-            def _():
-                pltpu.make_async_remote_copy(
-                    src_ref=tx.at[to, pl.ds(0, rows)], dst_ref=rx.at[me, pl.ds(0, rows)],
-                    send_sem=a_send.at[k], recv_sem=a_recv.at[k, lax.rem(8 - dy, 8)],
-                    device_id=(group, zz, cc, h), device_id_type=MESH,
-                ).start()
-
-            @pl.when(itself)
-            def _():
-                rx[me] = tx[me]
+            pltpu.make_async_remote_copy(
+                src_ref=tx.at[to, pl.ds(0, rows)], dst_ref=rx.at[me, pl.ds(0, rows)],
+                send_sem=a_send.at[k], recv_sem=a_recv.at[k, lax.rem(8 - dy, 8)],
+                device_id=(group, zz, cc, h), device_id_type=MESH,
+            ).start()
+
+        for e in (4, 5, 2, 3, 6, 7, 1):
+            send(e)
+
+        @pl.when(dy != 0)
+        def _():
+            send(0)
+
+        @pl.when(dy == 0)
+        def _():
+            rx[me] = tx[me]
 
     def far_first(i):
         return lax.rem(jnp.where(lax.rem(i, 2) == 1, 4 - (i + 1) // 2, 4 + i // 2), 8)
@@ -465,6 +467,12 @@
         pack_columns(p1, tx0, group, cpl)
 
 
+    def aside_on(i):
+        arrived(z_recv.at[i - 1], REST)
+        rest_on(0, lax.rem(z + 4 - i, 4), 0, 0)
+
+    aside_on(1)
+    aside_on(3)
     pl.semaphore_wait(z_ready, 3)
     pl.semaphore_signal(c_ready, inc=1, device_id=twin, device_id_type=MESH)
     pl.semaphore_wait(c_ready, 1)
@@ -474,10 +482,7 @@
         dy = far_first(i)
         exchange_start(0, lax.rem(y + dy, 8), dy)
 
-    for i in range(1, 4):
-        arrived(z_recv.at[i - 1], REST)
-        rest_on(0, lax.rem(z + 4 - i, 4), 0, 0)
-
+    aside_on(2)
     weight = jnp.concatenate([rw[...], rw[...]], axis=1)
     turned[...] = of_rows(rot) * weight - centre
     stacked[640:768] = jnp.zeros((128, 128), jnp.float32)
@@ -535,7 +540,6 @@
     ring_rest(3)
     compute(2)
     compute(-2)
-    ring_rest(4)
 
     @pl.loop(0, 8)
     def _(dy):
@@ -546,6 +550,7 @@
 
     compute(3)
     compute(-3)
+    ring_rest(4)
     compute(4)
 
     acc[NB:128] = jnp.zeros((128 - NB, J), jnp.float32)

time: 105 us -> 103 us (0.981)
  the two profiles are of different devices: /device:TPU:15 before, /device:TPU:23 now
where the time goes in v4:
time: 103 us
  Pallas kernels  102 us (99%)
    pallas_call x1, Pallas kernels, shards(): pl.pallas_call(kernel, out_shape=(whole, whole), in_specs=[vmem] * 10, ou...  100 us

profile of v4, /device:TPU:23, one launch (start us, length us, event | category | flops | bytes accessed | tf_op | source)
XLA Modules:
  0.0 102.8 jit_solution(15850728349693968349)
XLA Ops:
  0.6 100.3 %shard_map.113 = (f32[16,5120]{1,0:T(8,128)}, f32[16,5120]{1,0:T(8,128)}) custom-call(f32[16,5120]{1,0:T(8,128)} %bitcast.11, f32[16,5120]{1,0:T(8,128)} %bitcast.12, f32[24,1024]{1,0:T(8,128)} %bitcast.15, f32[80,1536]{1,0:T(8,128)} %bitcast.10, f32[1,16]{1,0:T(1,128)} %rot.1, f32[1,64]{1,0:T(1,128)} %bitcast.16, f32[1,16]{1,0:T(1,128)} %cpl.1, ...), custom_call_target="tpu_custom_call" | custom-call | flops 3019898880 | bytes 4194304 | tf_op jit(solution)/shard_map/pallas_call | solution.py:632
  100.9 1.9 %shard_map.114 = (f32[16,5120]{1,0:T(8,128)}, f32[16,5120]{1,0:T(8,128)}) custom-call(f32[16,5120]{1,0:T(8,128)} %get-tuple-element.6.mid, f32[16,5120]{1,0:T(8,128)} %get-tuple-element.7.last), custom_call_target="tpu_custom_call" | custom-call | tf_op jit(solution)/shard_map/pallas_call | solution.py:681

commit v5 on v4

--- a/solution.py
+++ b/solution.py
@@ -597,7 +597,8 @@
 
     def take_back(k, out):
         @pl.loop(0, 8)
-        def _(dy):
+        def _(i):
+            dy = far_first(i)
             exchange_wait(k, dy)
             group = lax.rem(y + dy, 8)
             for t, tile in enumerate(unpack_columns(rxs[k], group)):

time: 103 us -> 102 us (level)
  the two profiles are of different devices: /device:TPU:23 before, /device:TPU:15 now
where the time goes in v5:
time: 102 us
  Pallas kernels  102 us (100%)
    pallas_call x1, Pallas kernels, shards(): pl.pallas_call(kernel, out_shape=(whole, whole), in_specs=[vmem] * 10, ou...  99.8 us

profile of v5, /device:TPU:15, one launch (start us, length us, event | category | flops | bytes accessed | tf_op | source)
XLA Modules:
  0.0 102.3 jit_solution(7887787143509676031)
XLA Ops:
  0.6 99.8 %shard_map.113 = (f32[16,5120]{1,0:T(8,128)}, f32[16,5120]{1,0:T(8,128)}) custom-call(f32[16,5120]{1,0:T(8,128)} %bitcast.11, f32[16,5120]{1,0:T(8,128)} %bitcast.12, f32[24,1024]{1,0:T(8,128)} %bitcast.15, f32[80,1536]{1,0:T(8,128)} %bitcast.10, f32[1,16]{1,0:T(1,128)} %rot.1, f32[1,64]{1,0:T(1,128)} %bitcast.16, f32[1,16]{1,0:T(1,128)} %cpl.1, ...), custom_call_target="tpu_custom_call" | custom-call | flops 3019898880 | bytes 4194304 | tf_op jit(solution)/shard_map/pallas_call | solution.py:633
  100.4 1.9 %shard_map.114 = (f32[16,5120]{1,0:T(8,128)}, f32[16,5120]{1,0:T(8,128)}) custom-call(f32[16,5120]{1,0:T(8,128)} %get-tuple-element.6.mid, f32[16,5120]{1,0:T(8,128)} %get-tuple-element.7.last), custom_call_target="tpu_custom_call" | custom-call | tf_op jit(solution)/shard_map/pallas_call | solution.py:682
